TPU v7x, 128 devices: a whole 4x4x4 slice. The times are simulated.
128 devices in a mesh: ctx: 32 (over y_lo, z, x), tp: 4 (over y_hi, core).
Axes of the slice: x: 4, y: 4 (y_hi: 2, y_lo: 2; y = y_hi * 2 + y_lo), z: 4, core: 2. Of those that a mesh axis runs over, the one named last changes fastest.
Arguments:
- signal: bfloat16 [256, 65536], P('tp', 'ctx'), may hold values from -6 to 6
- grad_out: bfloat16 [256, 65536], P('tp', 'ctx'), may hold values from -6 to 6
- long_filter: float32 [65536], P('ctx'), may hold values from -2 to 2, as said below
- short_filter: float32 [128], replicated, may hold values from -0.5 to 0.5
- long_skip: float32 [256], P('tp'), may hold values from 0.5 to 1.5
- short_skip: float32 [256], P('tp'), may hold values from 0.25 to 1.25
Outputs:
- signal_grad: bfloat16 [256, 65536], P('tp', 'ctx')
- long_grad: float32 [65536], P(('ctx', 'tp'))
- short_grad: float32 [128], replicated
Inputs may be any that keep to these rules, and one draw needn't show every extreme that they name: `long_filter`: one filter shared by all channels of the group.
All inputs are finite; a program needn't handle non-finite values.
Results may differ from a plain program's by a relative error of at most 0.00045.
Values may be sent and summed in bfloat16 or wider, within the bound.
A program may use at most 64 MiB of HBM per device.

v0:
```python
import math

import jax
import jax.numpy as jnp
from jax import lax
from jax.sharding import PartitionSpec as P

highest = lax.Precision.HIGHEST


def pick_factors(total_len):
    tail_list = []
    while total_len > 128 and total_len % 128 == 0:
        tail_list.append(128)
        total_len = total_len // 128
    return [total_len] + tail_list


def dft_table(total_len):
    indices = jnp.arange(total_len, dtype=jnp.int32)
    products = indices[:, None] * indices[None, :] % total_len
    angles = products.astype(jnp.float32) * (2.0 * math.pi / total_len)
    return (jnp.cos(angles), jnp.sin(angles))


def twiddle_table(outer_len, inner_len):
    outer_idx = jnp.arange(outer_len, dtype=jnp.int32)
    inner_idx = jnp.arange(inner_len, dtype=jnp.int32)
    products = outer_idx[:, None] * inner_idx[None, :] % (outer_len * inner_len)
    angles = products.astype(jnp.float32) * (2.0 * math.pi / (outer_len * inner_len))
    return (jnp.cos(angles), jnp.sin(angles))


def rotate(re_part, im_part, cosine, sine_part, direction):
    return (
        cosine * re_part + direction * sine_part * im_part,
        cosine * im_part - direction * sine_part * re_part,
    )


def mix_rows(cosine, sine_part, re_part, im_part, direction):

    def apply_table(weights, values):
        return jnp.einsum("kn,...nb->...kb", weights, values, precision=highest)

    if im_part is None:
        return (apply_table(cosine, re_part), -direction * apply_table(sine_part, re_part))
    return (
        apply_table(cosine, re_part) + direction * apply_table(sine_part, im_part),
        apply_table(cosine, im_part) - direction * apply_table(sine_part, re_part),
    )


def mix_last(cosine, sine_part, re_part, im_part, direction):

    def apply_table(values, weights):
        return jnp.matmul(values, weights, precision=highest)

    return (
        apply_table(re_part, cosine) + direction * apply_table(im_part, sine_part),
        apply_table(im_part, cosine) - direction * apply_table(re_part, sine_part),
    )


def transform(re_part, im_part, factors, direction):
    total_len = re_part.shape[-1]
    leading = re_part.shape[:-1]
    if len(factors) == 1:
        cosine, sine_part = dft_table(total_len)
        return mix_last(cosine, sine_part, re_part, im_part, direction)
    outer_len = factors[0]
    inner_len = total_len // outer_len
    re_part = re_part.reshape(leading + (outer_len, inner_len))
    if im_part is not None:
        im_part = im_part.reshape(leading + (outer_len, inner_len))
    cos_twist, sin_twist = twiddle_table(outer_len, inner_len)
    cosine, sine_part = dft_table(outer_len)
    if direction > 0:
        re_part, im_part = mix_rows(cosine, sine_part, re_part, im_part, direction)
        re_part, im_part = rotate(re_part, im_part, cos_twist, sin_twist, direction)
        re_part, im_part = transform(re_part, im_part, factors[1:], direction)
    else:
        re_part, im_part = transform(re_part, im_part, factors[1:], direction)
        re_part, im_part = rotate(re_part, im_part, cos_twist, sin_twist, direction)
        re_part, im_part = mix_rows(cosine, sine_part, re_part, im_part, direction)
    return (re_part.reshape(leading + (total_len,)), im_part.reshape(leading + (total_len,)))


def times_spec(left_re, left_im, right_re, right_im):
    return (left_re * right_re - left_im * right_im, left_re * right_im + left_im * right_re)


def times_conj(left_re, left_im, right_re, right_im):
    return (left_re * right_re + left_im * right_im, left_im * right_re - left_re * right_im)


def band_table(short_filter):
    taps_len = short_filter.shape[0]
    extended = jnp.concatenate([short_filter, jnp.zeros((taps_len + 1,), jnp.float32)])
    tiled = jnp.tile(extended, taps_len)[: taps_len * 2 * taps_len]
    return tiled.reshape(taps_len, 2 * taps_len).T


def shards(signal, grad_out, long_filter, short_filter, long_skip, short_skip):
    n_ctx = lax.axis_size("ctx")
    per_device = signal.shape[0] // n_ctx
    chan_start = lax.axis_index("ctx") * per_device
    long_gain = lax.dynamic_slice_in_dim(long_skip, chan_start, per_device)[:, None]
    short_gain = lax.dynamic_slice_in_dim(short_skip, chan_start, per_device)[:, None]
    whole_filter = lax.all_gather(long_filter, "ctx", axis=0, tiled=True)
    sig_local, cot_local = (
        lax.all_to_all(signal, "ctx", split_axis=0, concat_axis=1, tiled=True),
        lax.all_to_all(grad_out, "ctx", split_axis=0, concat_axis=1, tiled=True),
    )
    seq_len = sig_local.shape[1]
    padded_len = 2 * seq_len
    factors = pick_factors(padded_len)
    scale_back = 1.0 / padded_len

    def padded(values):
        return jnp.concatenate([values, jnp.zeros(values.shape, jnp.float32)], axis=-1)

    def to_time(re_part, im_part):
        return transform(re_part, im_part, factors, -1)[0][..., :seq_len] * scale_back

    sig_wide = sig_local.astype(jnp.float32)
    cot_wide = cot_local.astype(jnp.float32)
    filt_re, filt_im = transform(padded(whole_filter[None, :]), None, factors, 1)
    sig_re, sig_im = transform(padded(sig_wide), None, factors, 1)
    hid_re, hid_im = times_spec(sig_re, sig_im, filt_re, filt_im)
    hidden = to_time(hid_re, hid_im) + long_gain * sig_wide
    taps_len = short_filter.shape[0]
    block_count = seq_len // taps_len
    cot_blocks = cot_wide.reshape(per_device, block_count, taps_len)
    next_blocks = jnp.concatenate(
        [cot_blocks[:, 1:], jnp.zeros((per_device, 1, taps_len), jnp.float32)], axis=1
    )
    cot_pairs = jnp.concatenate([cot_blocks, next_blocks], axis=2)
    toeplitz = band_table(short_filter)
    back_short = jnp.einsum("cbm,mi->cbi", cot_pairs, toeplitz, precision=highest).reshape(
        per_device, seq_len
    )
    back_short = back_short + short_gain * cot_wide
    hid_blocks = hidden.reshape(per_device, block_count, taps_len)
    prev_blocks = jnp.concatenate(
        [jnp.zeros((per_device, 1, taps_len), jnp.float32), hid_blocks[:, :-1]], axis=1
    )
    hid_pairs = jnp.concatenate([prev_blocks, hid_blocks], axis=2)
    cross = jnp.einsum("cbi,cbm->im", cot_blocks, hid_pairs, precision=highest)
    row_idx = jnp.arange(taps_len, dtype=jnp.int32)[:, None, None]
    col_idx = jnp.arange(2 * taps_len, dtype=jnp.int32)[None, :, None]
    lag_idx = jnp.arange(taps_len, dtype=jnp.int32)[None, None, :]
    selector = (col_idx == taps_len + row_idx - lag_idx).astype(jnp.float32)
    tap_terms = jnp.einsum("im,imj->j", cross, selector, precision=highest)
    short_grad = lax.psum(tap_terms, ("ctx", "tp"))
    back_re, back_im = transform(padded(back_short), None, factors, 1)
    grad_re, grad_im = times_conj(back_re, back_im, filt_re, filt_im)
    sig_grad = (to_time(grad_re, grad_im) + long_gain * back_short).astype(jnp.bfloat16)
    corr_re, corr_im = times_conj(back_re, back_im, sig_re, sig_im)
    filter_terms = to_time(jnp.sum(corr_re, axis=0), jnp.sum(corr_im, axis=0))
    signal_grad = lax.all_to_all(sig_grad, "ctx", split_axis=1, concat_axis=0, tiled=True)
    long_grad = lax.psum_scatter(filter_terms, ("ctx", "tp"), scatter_dimension=0, tiled=True)
    return (signal_grad, long_grad, short_grad)


def solution(mesh):
    placed = (P("tp", "ctx"), P("tp", "ctx"), P("ctx"), P(), P("tp"), P("tp"))
    return jax.shard_map(
        shards,
        mesh=mesh,
        in_specs=placed,
        out_specs=(P("tp", "ctx"), P(("ctx", "tp")), P()),
        check_vma=False,
    )
```

profile of v0, /device:TPU:1, one launch (start us, length us, event | category | flops | bytes accessed | tf_op | source)
XLA Modules:
  0.0 433.7 jit_solution(6242923394050453460)
XLA Ops:
  9.0 9.9 %all-to-all-start = ((bf16[32,2,2048]{2,1,0:T(2,128)(2,1)}), bf16[32,2,2048]{2,1,0:T(2,128)(2,1)}, u32[]{:S(2)}, u32[]{:S(2)}) async-start(bf16[32,2,2048]{2,1,0:T(2,128)(2,1)} %all_to_all.38), calls=%async_computation | async-start | bytes 524288 | tf_op jit(solution)/shard_map/all_to_all | solution.py:113
  18.9 2.9 broadcast_multiply_fusion
  21.8 2.9 fusion.114
  27.5 68.9 %all_gather.3 = f32[65536]{0:T(1024)S(1)} all-gather(f32[2048]{0:T(1024)S(1)} %copy-done.39), channel_id=1, replica_groups=mesh['ctx'=32,'tp'=4] {'ctx'}, dimensions={0}, use_global_device_ids=true | all-gather | bytes 270336 | tf_op jit(solution)/shard_map/all_gather | solution.py:110
  98.0 2.6 subtract_bitcast_fusion.2
  109.3 4.8 %all-to-all-start.2 = ((bf16[32,2,2048]{2,1,0:T(2,128)(2,1)}), bf16[32,2,2048]{2,1,0:T(2,128)(2,1)}, u32[]{:S(2)}, u32[]{:S(2)}) async-start(bf16[32,2,2048]{2,1,0:T(2,128)(2,1)} %all_to_all.46), calls=%async_computation.2 | async-start | bytes 524288 | tf_op jit(solution)/shard_map/all_to_all | solution.py:112
  130.9 3.7 subtract_bitcast_fusion.1
  142.8 3.0 fusion.102
  145.8 3.0 fusion.103
  148.8 2.6 copy.198
  151.3 3.4 fusion.168
  154.8 2.6 copy.197
  157.3 3.0 fusion.170
  208.3 3.1 fusion.24
  213.5 3.8 fusion.68
  217.3 5.0 %fusion.65 = f32[8,16384]{1,0:T(8,128)} fusion(f32[1,8,128,128]{3,2,1,0:T(8,128)} %bitcast.314, f32[1,8,128,128]{3,2,1,0:T(8,128)S(1)} %bitcast.312), kind=kOutput, calls=%fused_computation.131 | convolution fusion | flops 14943104 | bytes 1572864 | tf_op jit(solution)/shard_map/kn,...nb->...kb/dot_general | solution.py:44
  227.2 4.0 fusion.16
  231.2 2.5 reshape.379
  233.7 2.8 fusion.50
  244.4 3.7 fusion.8
  255.3 5.5 %all-to-all-start.1 = ((bf16[2,32,2048]{2,0,1:T(2,128)(2,1)}), bf16[2,32,2048]{2,0,1:T(2,128)(2,1)S(1)}, u32[]{:S(2)}, u32[]{:S(2)}) async-start(bf16[2,32,2048]{2,0,1:T(2,128)(2,1)} %bitcast.38), calls=%async_computation.1 | async-start | bytes 524288 | tf_op jit(solution)/shard_map/all_to_all | solution.py:161
  262.5 5.4 %fusion.31 = f32[128]{0:T(128)S(1)} fusion(f32[128,256,1]{1,2,0:T(1,128)S(1)} %copy.255, s32[128,128]{1,0:T(8,128)S(1)} %iota_subtract_fusion), kind=kOutput, calls=%fused_computation.66 | convolution fusion | flops 54525952 | bytes 197120 | tf_op jit(solution)/shard_map/im,imj->j/dot_general | solution.py:154
  267.9 80.4 %psum.7 = f32[128]{0:T(128)} all-reduce(f32[128]{0:T(128)S(1)} %fusion.31), channel_id=1, replica_groups=mesh['ctx'=32,'tp'=4] {'ctx','tp'}, use_global_device_ids=true, to_apply=%region_3.4 | all-reduce | flops 128 | bytes 1024 | tf_op jit(solution)/shard_map/psum | solution.py:155
  348.3 76.2 %all-reduce.9.cloned.1.call-done = f32[65536]{0:T(1024)} async-done(((f32[65536]{0:T(1024)}), f32[65536]{0:T(1024)}) %all-reduce.9.cloned.1.call-update) | async-done | bytes 262160
  (186 shorter events, 112.8 us)
Async XLA Ops:
  9.0 100.3 %all-to-all-start = ((bf16[32,2,2048]{2,1,0:T(2,128)(2,1)}), bf16[32,2,2048]{2,1,0:T(2,128)(2,1)}, u32[]{:S(2)}, u32[]{:S(2)}) async-start(bf16[32,2,2048]{2,1,0:T(2,128)(2,1)} %all_to_all.38), calls=%async_computation | async-start | bytes 524288 | tf_op jit(solution)/shard_map/all_to_all | solution.py:113
  18.9 6.4 %copy-start.40 = (f32[128]{0:T(128)S(1)}, f32[128]{0:T(128)}, u32[]{:S(2)}) copy-start(f32[128]{0:T(128)} %param.9) | copy-start | bytes 1540
  21.8 109.1 %copy-start.4 = (f32[8,16384]{1,0:T(8,128)}, f32[8,16384]{1,0:T(8,128)S(1)}, u32[]{:S(2)}) copy-start(f32[8,16384]{1,0:T(8,128)S(1)} %get-tuple-element.17) | copy-start | bytes 1572868
  21.8 4.6 %copy-start.36 = (bf16[64,2048]{1,0:T(8,128)(2,1)S(1)}, bf16[64,2048]{1,0:T(8,128)(2,1)}, u32[]{:S(2)}) copy-start(bf16[64,2048]{1,0:T(8,128)(2,1)} %param.6) | copy-start | bytes 786436
  24.7 106.2 %copy-start.6 = (f32[8,16384]{1,0:T(8,128)}, f32[8,16384]{1,0:T(8,128)S(1)}, u32[]{:S(2)}) copy-start(f32[8,16384]{1,0:T(8,128)S(1)} %get-tuple-element.19) | copy-start | bytes 1572868
  24.7 2.8 copy-start.39
  109.3 12.3 %all-to-all-start.2 = ((bf16[32,2,2048]{2,1,0:T(2,128)(2,1)}), bf16[32,2,2048]{2,1,0:T(2,128)(2,1)}, u32[]{:S(2)}, u32[]{:S(2)}) async-start(bf16[32,2,2048]{2,1,0:T(2,128)(2,1)} %all_to_all.46), calls=%async_computation.2 | async-start | bytes 524288 | tf_op jit(solution)/shard_map/all_to_all | solution.py:112
  135.0 2.5 copy-start.9
  157.3 3.0 copy-start.11
  157.3 3.0 copy-start.19
  179.8 4.0 copy-start
  213.4 3.8 copy-start.33
  213.4 8.9 %copy-start.24 = (f32[2,8,128,128]{2,3,1,0:T(8,128)S(1)}, f32[2,8,128,128]{2,3,1,0:T(8,128)}, u32[]{:S(2)}) copy-start(f32[2,8,128,128]{2,3,1,0:T(8,128)} %fusion.104) | copy-start | bytes 3145732
  217.3 5.1 %copy-start.1 = (f32[2,8,128,128]{2,3,1,0:T(8,128)S(1)}, f32[2,8,128,128]{2,3,1,0:T(8,128)}, u32[]{:S(2)}) copy-start(f32[2,8,128,128]{2,3,1,0:T(8,128)} %copy-done) | copy-start | bytes 3145732
  217.3 5.1 %copy-start.3 = (f32[2,8,128,128]{2,3,1,0:T(8,128)S(1)}, f32[2,8,128,128]{2,3,1,0:T(8,128)}, u32[]{:S(2)}) copy-start(f32[2,8,128,128]{2,3,1,0:T(8,128)} %copy-done.2) | copy-start | bytes 3145732
  231.2 2.5 copy-start.5
  231.2 2.5 copy-start.7
  233.7 2.8 copy-start.13
  233.7 2.8 copy-start.14
  255.1 5.8 %copy-start.37 = (f32[8,16384]{1,0:T(8,128)S(1)}, f32[8,16384]{1,0:T(8,128)}, u32[]{:S(2)}) copy-start(f32[8,16384]{1,0:T(8,128)} %fusion.68) | copy-start | bytes 1572868
  255.1 5.8 %copy-start.38 = (f32[8,16384]{1,0:T(8,128)S(1)}, f32[8,16384]{1,0:T(8,128)}, u32[]{:S(2)}) copy-start(f32[8,16384]{1,0:T(8,128)} %fusion.65) | copy-start | bytes 1572868
  255.1 5.8 %copy-start.22 = (bf16[2,512,128]{2,1,0:T(8,128)(2,1)S(1)}, bf16[2,512,128]{2,1,0:T(8,128)(2,1)}, u32[]{:S(2)}) copy-start(bf16[2,512,128]{2,1,0:T(8,128)(2,1)} %copy-done.21) | copy-start | bytes 786436
  255.3 170.5 %all-to-all-start.1 = ((bf16[2,32,2048]{2,0,1:T(2,128)(2,1)}), bf16[2,32,2048]{2,0,1:T(2,128)(2,1)S(1)}, u32[]{:S(2)}, u32[]{:S(2)}) async-start(bf16[2,32,2048]{2,0,1:T(2,128)(2,1)} %bitcast.38), calls=%async_computation.1 | async-start | bytes 524288 | tf_op jit(solution)/shard_map/all_to_all | solution.py:161
  260.8 163.7 %all-reduce.9.cloned.1.call-start = ((), (), s32[]{:S(2)}) async-start(), calls=%async_computation.3 | async-start | bytes 524288
  (23 other events, 37.1 us)
Sparse Core Ops, SparseCore 0:
  266.3 158.1 all-reduce.8
where the time goes:
time: 438 us; the launch traced here: 434 us
  blocking collectives  149 us (34%)
  matrix products  124 us (28%)
  waiting for transfers between devices  78.6 us (18%)
  local copies, waits for them, and re-layouts  35 us (8%)
  starting transfers between devices  20.1 us (5%)
  between operations  15.3 us (3%)
  other arithmetic  11.5 us (3%)
    psum x1, blocking collectives, shards(): short_grad = lax.psum(tap_terms, ('ctx', 'tp'))  80.4 us
    dot_general x36, matrix products, apply_table(): return jnp.einsum('kn,...nb->...kb', weights, values, precision=highest)  76.3 us
    unnamed x2, waiting for transfers between devices  76.2 us
    all_gather x1, blocking collectives, shards(): whole_filter = lax.all_gather(long_filter, 'ctx', axis=0, tiled=True)  68.9 us
    dot_general x24, matrix products, apply_table(): return jnp.matmul(values, weights, precision=highest)  40.4 us
    all_to_all x1, starting transfers between devices, shards(): lax.all_to_all(grad_out, 'ctx', split_axis=0, concat_axis=1, tiled=True)  9.85 us
  transfers between devices with their start and end apart: 4, of which 2 were waited for; matrix products, arithmetic and copies ran while one was open for 8% of the time, Pallas kernels for 0%

commit v1 on v0

v1 whole, which is shorter than its diff:
```python
import math

import jax
import jax.numpy as jnp
import ml_dtypes
import numpy as np
from jax import lax
from jax.experimental import pallas as pl
from jax.experimental.pallas import tpu as pltpu
from jax.sharding import PartitionSpec as P

MESH = pl.DeviceIdType.MESH
F32, BF16 = jnp.float32, jnp.bfloat16
N1, N2 = 512, 128
LEN = N1 * N2


def split_np(x):
    x = x.astype(np.float32)
    hi = x.astype(ml_dtypes.bfloat16)
    lo = (x - hi.astype(np.float32)).astype(ml_dtypes.bfloat16)
    return hi, lo


def tables():
    k = np.arange(N1, dtype=np.float64)[:, None] + 0.25
    n = np.arange(N1, dtype=np.float64)[None, :]
    ang = -2 * np.pi * np.mod(k * n, N1) / N1
    fwd = np.concatenate([np.cos(ang), np.sin(ang)], axis=0)
    f_hi, f_lo = split_np(fwd)
    f_cat = np.concatenate([f_hi, f_lo], axis=1)
    i_hi, i_lo = np.ascontiguousarray(f_hi.T), np.ascontiguousarray(f_lo.T)
    i_cat = np.concatenate([i_hi, i_lo], axis=1)
    m = np.arange(N2, dtype=np.float64)
    ang = -2 * np.pi * k * m[None, :] / LEN
    twist = np.concatenate([np.cos(ang), np.sin(ang)], axis=1).astype(np.float32)
    ang = -2 * np.pi * np.mod(m[:, None] * m[None, :], N2) / N2
    br, bi = np.cos(ang), np.sin(ang)
    b_hi, b_lo = split_np(np.block([[br, bi], [-bi, br]]))
    b_cat = np.concatenate([b_hi, b_hi, b_lo], axis=0)
    c_hi, c_lo = split_np(np.block([[br, -bi], [bi, br]]) / LEN)
    c_cat = np.concatenate([c_hi, c_hi, c_lo], axis=0)
    return f_cat, i_cat, twist, b_cat, c_cat


def dot(a, b):
    return jnp.dot(a, b, preferred_element_type=F32)


def split(x):
    hi = x.astype(BF16)
    return hi, (x - hi.astype(F32)).astype(BF16)


def split3(x):
    hi, lo = split(x)
    return jnp.concatenate([hi, lo, hi], axis=1)


def rows_of(i, size):
    return pl.ds(pl.multiple_of(i * size, size), size)


def twist_and_mix(yr, yi, tw, b_cat):
    tr, ti = tw[:, :N2], tw[:, N2:]
    y = jnp.concatenate([yr * tr - yi * ti, yi * tr + yr * ti], axis=1)
    return dot(split3(y), b_cat)


def forward_exact(x, f_cat, twist, b_cat, z_refs, block=128):
    x2 = jnp.concatenate([x, x], axis=0)

    def step(i, carry):
        r = rows_of(i, block)
        yr = dot(f_cat[r, :], x2)
        yi = dot(f_cat[pl.ds(pl.multiple_of(N1 + i * block, block), block), :], x2)
        tw = twist[r, :]
        for q, z in enumerate(z_refs):
            s = slice(q * N2, (q + 1) * N2)
            z[r, :] = twist_and_mix(yr[:, s], yi[:, s], tw, b_cat[...])
        return carry

    lax.fori_loop(0, N1 // block, step, 0)


def forward_split(hi, lo, f_cat, twist, b_cat, z_refs, block=128):
    x2 = jnp.concatenate([hi, hi], axis=0)

    def step(i, carry):
        r = rows_of(i, block)
        ri = pl.ds(pl.multiple_of(N1 + i * block, block), block)
        yr = dot(f_cat[r, :], x2) + dot(f_cat[r, :N1], lo)
        yi = dot(f_cat[ri, :], x2) + dot(f_cat[ri, :N1], lo)
        tw = twist[r, :]
        for q, z in enumerate(z_refs):
            s = slice(q * N2, (q + 1) * N2)
            z[r, :] = twist_and_mix(yr[:, s], yi[:, s], tw, b_cat[...])
        return carry

    lax.fori_loop(0, N1 // block, step, 0)


def inverse_pair(left, right, i_cat, twist, c_cat, y_hi, y_lo, out, block=128):
    def step(i, carry):
        r = rows_of(i, block)
        ri = pl.ds(pl.multiple_of(N1 + i * block, block), block)
        tr, ti = twist[r, :N2], twist[r, N2:]
        for c in range(2):
            ar, ai = left[c][r, :N2], left[c][r, N2:]
            br, bi = right[c][r, :N2], right[c][r, N2:]
            z = jnp.concatenate([ar * br + ai * bi, ai * br - ar * bi], axis=1)
            y = dot(split3(z), c_cat[...])
            yr, yi = y[:, :N2], y[:, N2:]
            s = slice(c * N2, (c + 1) * N2)
            y_hi[r, s], y_lo[r, s] = split(yr * tr + yi * ti)
            y_hi[ri, s], y_lo[ri, s] = split(yi * tr - yr * ti)
        return carry

    lax.fori_loop(0, N1 // block, step, 0)
    hi2 = jnp.concatenate([y_hi[...], y_hi[...]], axis=0)

    def final(i, carry):
        r = rows_of(i, block)
        out[r, :] = dot(i_cat[r, :], hi2) + dot(i_cat[r, : 2 * N1], y_lo[...])
        return carry

    lax.fori_loop(0, N1 // block, final, 0)


def dot3(a, b):
    ah, al = split(a)
    bh, bl = split(b)
    return dot(ah, bh) + (dot(ah, bl) + dot(al, bh))


def dot3_nt(a, b):
    def nt(x, y):
        return lax.dot_general(x, y, (((1,), (1,)), ((), ())), preferred_element_type=F32)

    ah, al = split(a)
    bh, bl = split(b)
    return nt(ah, bh) + (nt(ah, bl) + nt(al, bh))


def swap_matrix():
    i = lax.broadcasted_iota(jnp.int32, (256, 256), 0)
    j = lax.broadcasted_iota(jnp.int32, (256, 256), 1)
    same = (i // 16 == j % 16) & (i % 16 == j // 16)
    return jnp.where(same, 1.0, 0.0).astype(BF16)


def long_and_short(r_buf, corr, f_buf, w_row, alpha, lam):
    r0, r1 = corr[:, :N2], corr[:, N2:]
    r_sum = r0 + r1
    r_buf[:N1, :] = r_sum
    r_pair = jnp.concatenate([r_sum, r_buf[pl.ds(1, N1), :]], axis=1)
    zero = jnp.zeros((1, N2), F32)
    base = jnp.broadcast_to(jnp.concatenate([w_row, zero], axis=1), (N2, 2 * N2))
    toep = pltpu.roll(base, 0, 1, stride=1, stride_axis=0)
    long = dot3_nt(r_pair, toep) + (alpha[0] * r0 + alpha[1] * r1)
    cross = dot3(jnp.transpose(f_buf[8 : 8 + N1, :]), r_pair)
    i = lax.broadcasted_iota(jnp.int32, (N2, N2), 0)
    j = lax.broadcasted_iota(jnp.int32, (N2, N2), 1)
    flip = jnp.where(i + j == N2 - 1, 1.0, 0.0).astype(BF16)
    ch, cl = split(cross)
    back = dot(flip, ch) + dot(flip, cl)
    diag = pltpu.roll(back, N2 + 1, 1, stride=1, stride_axis=0)
    short = jnp.sum(diag, axis=0, keepdims=True)[:, :N2]
    return long, short + (lam[0] * r0[:1, :] + lam[1] * r1[:1, :])


def filters(f_buf, w_row, alpha, lam, v_hi, v_lo):
    f = f_buf[8 : 8 + N1, :]
    f_pair = jnp.concatenate([f_buf[pl.ds(7, N1), :], f], axis=1)
    zero = jnp.zeros((1, N2), F32)
    base = jnp.broadcast_to(jnp.concatenate([zero, w_row], axis=1), (2 * N2, 2 * N2))
    toep = pltpu.roll(base, 0, 1, stride=1, stride_axis=0)[:, :N2]
    u = dot3(f_pair, toep)
    first_row = lax.broadcasted_iota(jnp.int32, (8, N2), 0) == 0
    first = first_row & (lax.broadcasted_iota(jnp.int32, (8, N2), 1) == 0)
    for c in range(2):
        s = slice(c * N2, (c + 1) * N2)
        v = u + alpha[c] * f
        extra = jnp.where(first_row, lam[c] * w_row, 0.0) + jnp.where(first, lam[c] * alpha[c], 0.0)
        v = jnp.concatenate([v[:8] + extra, v[8:]], axis=0)
        v_hi[:, s], v_lo[:, s] = split(v)


def kernel(
    n_ctx, n_tp,
    sig, cot, filt, w_in, lam_in, alpha_in, f_tab, i_tab, t_tab, b_tab, c_tab,
    sg_out, long_out, short_out,
    sig_v, cot_v, filt_v, f_cat, i_cat, twist, b_cat, c_cat,
    send, recv, f_buf, zs0, zg0, zs1, zg1, y_hi, y_lo, corr, r_buf,
    l_send, l_recv, t_send, t_recv, v_hi, v_lo, zv0, zv1, sg_send, sg_recv,
    load_sem, tab_sem, send_sem, recv_sem,
):
    me, tp = lax.axis_index("ctx"), lax.axis_index("tp")

    def peer(i):
        return lax.rem(me + i, n_ctx)

    def tp_peer(i):
        return lax.rem(tp + i, n_tp)

    barrier = pltpu.get_barrier_semaphore()

    def greet(i, carry):
        pl.semaphore_signal(barrier, inc=1, device_id={"ctx": peer(i)}, device_id_type=MESH)
        return carry

    def greet_tp(i, carry):
        pl.semaphore_signal(barrier, inc=1, device_id={"tp": tp_peer(i)}, device_id_type=MESH)
        return carry

    loads = [
        pltpu.make_async_copy(src, dst, load_sem.at[i])
        for i, (src, dst) in enumerate([(sig, sig_v), (cot, cot_v), (filt, filt_v)])
    ]
    for c in loads:
        c.start()
    lax.fori_loop(1, n_ctx, greet, 0)
    lax.fori_loop(1, n_tp, greet_tp, 0)
    tabs = [
        pltpu.make_async_copy(src, dst, tab_sem.at[i])
        for i, (src, dst) in enumerate(
            [(f_tab, f_cat), (t_tab, twist), (b_tab, b_cat), (c_tab, c_cat), (i_tab, i_cat)]
        )
    ]
    for c in tabs:
        c.start()
    f_buf[:8, :] = jnp.zeros((8, N2), F32)
    r_buf[N1:, :] = jnp.zeros((8, N2), F32)
    swap = swap_matrix()
    for c in loads:
        c.wait()
    for g in range(4):
        ch = slice(16 * g, 16 * (g + 1))
        x = jnp.concatenate(
            [
                jnp.concatenate([v[ch, N2 * a : N2 * (a + 1)] for a in range(16)], axis=0)
                for v in (sig_v, cot_v)
            ],
            axis=1,
        )
        y = dot(swap, x).astype(BF16)
        send[ch, 0] = y[:, :N2].reshape(16, 16, N2)
        send[ch, 1] = y[:, N2:].reshape(16, 16, N2)
    pl.semaphore_wait(barrier, n_ctx + n_tp - 2)

    rows_me = pl.ds(pl.multiple_of(16 * me, 16), 16)

    def remote(src, dst, k, where):
        return pltpu.make_async_remote_copy(
            src_ref=src, dst_ref=dst, send_sem=send_sem.at[k], recv_sem=recv_sem.at[k],
            device_id=where, device_id_type=MESH,
        )

    def finish(ref, sem):
        pltpu.make_async_copy(ref, ref, sem).wait()

    def send_in(i, carry):
        e = peer(i)
        remote(send.at[pl.ds(2 * e, 2)], recv.at[:, :, rows_me, :], 0, {"ctx": e}).start()
        return carry

    def send_filter(i, carry):
        e = peer(i)
        remote(filt_v, f_buf.at[pl.ds(pl.multiple_of(8 + 16 * me, 8), 16), :], 1, {"ctx": e}).start()
        return carry

    pltpu.make_async_copy(send.at[pl.ds(2 * me, 2)], recv.at[:, :, rows_me, :], recv_sem.at[0]).start()
    pltpu.make_async_copy(
        filt_v, f_buf.at[pl.ds(pl.multiple_of(8 + 16 * me, 8), 16), :], recv_sem.at[1]
    ).start()
    lax.fori_loop(1, n_ctx, send_in, 0)
    lax.fori_loop(1, n_ctx, send_filter, 0)

    w_row = w_in[...]
    alpha = (alpha_in[2 * me], alpha_in[2 * me + 1])
    lam = (lam_in[2 * me], lam_in[2 * me + 1])
    for c in tabs:
        c.wait()

    finish(recv, recv_sem.at[0])
    x = jnp.concatenate([recv[0, 0], recv[0, 1], recv[1, 0], recv[1, 1]], axis=1)
    forward_exact(x, f_cat, twist, b_cat, (zs0, zg0, zs1, zg1))
    inverse_pair((zg0, zg1), (zs0, zs1), i_cat, twist, c_cat, y_hi, y_lo, corr)

    finish(f_buf.at[pl.ds(8, N1), :], recv_sem.at[1])
    long, short = long_and_short(r_buf, corr, f_buf, w_row, alpha, lam)
    l_send[:, :16, :] = long.reshape(32, 16, N2)
    l_send[:, 16:, :] = jnp.broadcast_to(short.reshape(1, 1, N2), (32, 8, N2))

    def send_long(i, carry):
        e = peer(i)
        remote(l_send.at[e], l_recv.at[me], 2, {"ctx": e}).start()
        return carry

    pltpu.make_async_copy(l_send.at[me], l_recv.at[me], recv_sem.at[2]).start()
    lax.fori_loop(1, n_ctx, send_long, 0)

    filters(f_buf, w_row, alpha, lam, v_hi, v_lo)
    forward_split(v_hi[...], v_lo[...], f_cat, twist, b_cat, (zv0, zv1))
    inverse_pair((zg0, zg1), (zv0, zv1), i_cat, twist, c_cat, y_hi, y_lo, corr)
    sg_send[0] = corr[:, :N2].astype(BF16)
    sg_send[1] = corr[:, N2:].astype(BF16)

    def send_back(i, carry):
        e = peer(i)
        rows = pl.ds(pl.multiple_of(16 * e, 16), 16)
        remote(sg_send.at[:, rows, :], sg_recv.at[pl.ds(2 * me, 2)], 4, {"ctx": e}).start()
        return carry

    pltpu.make_async_copy(
        sg_send.at[:, rows_me, :], sg_recv.at[pl.ds(2 * me, 2)], recv_sem.at[4]
    ).start()
    lax.fori_loop(1, n_ctx, send_back, 0)

    finish(l_recv, recv_sem.at[2])
    total = l_recv[0]
    for d in range(1, 32):
        total = total + l_recv[d]
    for t in range(4):
        t_send[t, :4, :] = total[4 * t : 4 * (t + 1)]
        t_send[t, 4:, :] = total[16:20]

    def send_tp(i, carry):
        t = tp_peer(i)
        remote(t_send.at[t], t_recv.at[tp], 3, {"tp": t}).start()
        return carry

    pltpu.make_async_copy(t_send.at[tp], t_recv.at[tp], recv_sem.at[3]).start()
    lax.fori_loop(1, n_tp, send_tp, 0)

    finish(sg_recv, recv_sem.at[4])
    for g in range(2):
        x = jnp.concatenate(
            [sg_recv[32 * g + 16 * h : 32 * g + 16 * (h + 1)].reshape(256, N2) for h in range(2)], axis=1
        )
        y = dot(swap, x).astype(BF16)
        for h in range(2):
            ch = slice(32 * g + 16 * h, 32 * g + 16 * (h + 1))
            for a in range(16):
                sg_out[ch, N2 * a : N2 * (a + 1)] = y[16 * a : 16 * (a + 1), h * N2 : (h + 1) * N2]
    finish(t_recv, recv_sem.at[3])
    whole = (t_recv[0] + t_recv[1]) + (t_recv[2] + t_recv[3])
    long_out[...] = whole[:4]
    short_out[...] = whole[4:5]
    finish(send.at[pl.ds(0, 62)], send_sem.at[0])
    finish(f_buf.at[pl.ds(8, 16 * 31), :], send_sem.at[1])
    finish(l_send.at[pl.ds(0, 31)], send_sem.at[2])
    finish(t_send.at[pl.ds(0, 3)], send_sem.at[3])
    finish(sg_recv.at[pl.ds(0, 62)], send_sem.at[4])


def shards(signal, grad_out, long_filter, short_filter, long_skip, short_skip):
    n_ctx, n_tp = lax.axis_size("ctx"), lax.axis_size("tp")
    consts = [jnp.asarray(t) for t in tables()]
    any_spec = pl.BlockSpec(memory_space=pl.ANY)
    vmem = pl.BlockSpec(memory_space=pltpu.VMEM)
    smem = pl.BlockSpec(memory_space=pltpu.SMEM)
    V = pltpu.VMEM
    spec = V((N1, 2 * N2), F32)
    sg, long, short = pl.pallas_call(
        lambda *refs: kernel(n_ctx, n_tp, *refs),
        out_shape=(
            jax.ShapeDtypeStruct((64, 2048), BF16),
            jax.ShapeDtypeStruct((4, N2), F32),
            jax.ShapeDtypeStruct((1, N2), F32),
        ),
        in_specs=[any_spec] * 3 + [vmem, smem, smem] + [any_spec] * 5,
        out_specs=(vmem, vmem, vmem),
        scratch_shapes=[
            V((64, 2048), BF16), V((64, 2048), BF16), V((16, N2), F32),
            V((1024, 1024), BF16), V((512, 2048), BF16), V((N1, 2 * N2), F32),
            V((768, 256), BF16), V((768, 256), BF16),
            V((64, 2, 16, N2), BF16), V((2, 2, N1, N2), BF16), V((N1 + 8, N2), F32),
            spec, spec, spec, spec,
            V((2 * N1, 2 * N2), BF16), V((2 * N1, 2 * N2), BF16), spec, V((N1 + 8, N2), F32),
            V((32, 24, N2), F32), V((32, 24, N2), F32), V((4, 8, N2), F32), V((4, 8, N2), F32),
            V((N1, 2 * N2), BF16), V((N1, 2 * N2), BF16), spec, spec,
            V((2, N1, N2), BF16), V((64, 16, N2), BF16),
            pltpu.SemaphoreType.DMA((3,)), pltpu.SemaphoreType.DMA((5,)),
            pltpu.SemaphoreType.DMA((5,)), pltpu.SemaphoreType.DMA((5,)),
        ],
        compiler_params=pltpu.CompilerParams(
            collective_id=0, has_side_effects=True, vmem_limit_bytes=48 * 1024 * 1024
        ),
        cost_estimate=pl.CostEstimate(flops=6_000_000_000, bytes_accessed=8_000_000, transcendentals=0),
    )(
        signal, grad_out, long_filter.reshape(16, N2), short_filter.reshape(1, N2),
        long_skip, short_skip, *consts,
    )
    return sg, long.reshape(512), short.reshape(N2)


def solution(mesh):
    placed = (P("tp", "ctx"), P("tp", "ctx"), P("ctx"), P(), P("tp"), P("tp"))
    return jax.shard_map(
        shards,
        mesh=mesh,
        in_specs=placed,
        out_specs=(P("tp", "ctx"), P(("ctx", "tp")), P()),
        check_vma=False,
    )
```

time: 438 us -> 50 us (0.11)
  blocking collectives: 149 us -> 0 us
  matrix products: 124 us -> 0 us
  waiting for transfers between devices: 78.6 us -> 0 us
  Pallas kernels: 0 us -> 37.4 us
  local copies, waits for them, and re-layouts: 35 us -> 11 us
  starting transfers between devices: 20.1 us -> 0 us
  between operations: 15.3 us -> 0.66 us
  other arithmetic: 11.5 us -> 0 us
    dot_general x63 -> x0, matrix products: 124 us -> none  [the longest x36 76.3 us: apply_table(): return jnp.einsum('kn,...nb->...kb', weights, values, precision=highest)]
    psum x1 -> x0, blocking collectives: 80.4 us -> none  [shards(): short_grad = lax.psum(tap_terms, ('ctx', 'tp'))]
    unnamed x2 -> x0, waiting for transfers between devices: 76.2 us -> none
    all_gather x1 -> x0, blocking collectives: 68.9 us -> none  [shards(): whole_filter = lax.all_gather(long_filter, 'ctx', axis=0, tiled=True)]
    pallas_call x0 -> x1, Pallas kernels: none -> 37.4 us  [shards(): pl.pallas_call(lambda *refs: kernel(n_ctx, n_tp, *refs), out_shape=(jax.S...]
    all_to_all x3 -> x0, starting transfers between devices: 20.1 us -> none  [the longest x1 9.85 us: shards(): lax.all_to_all(grad_out, 'ctx', split_axis=0, concat_axis=1, tiled=True)]
    reshape x10 -> x0, local copies, waits for them, and re-layouts: 16.7 us -> none  [the longest x2 4.81 us: transform(): re_part.reshape(leading + (total_len,))]
    all_to_all x5 -> x0, local copies, waits for them, and re-layouts: 4.72 us -> none  [the longest x3 2.99 us: shards(): lax.all_to_all(grad_out, 'ctx', split_axis=0, concat_axis=1, tiled=True)]
  transfers between devices with their start and end apart: 4 -> 0, of which waited for: 2 -> 0; matrix products, arithmetic and copies ran while one was open for 8% -> 0% of each run, Pallas kernels for 0% -> 0%
where the time goes in v1:
time: 50 us; the launch traced here: 49 us
  Pallas kernels  37.4 us (75%)
  local copies, waits for them, and re-layouts  11 us (22%)
  between operations  0.66 us (1%)
    pallas_call x1, Pallas kernels, shards(): pl.pallas_call(lambda *refs: kernel(n_ctx, n_tp, *refs), out_shape=(jax.S...  37.4 us
    unnamed x23, local copies, waits for them, and re-layouts  11 us

profile of v1, /device:TPU:1, one launch (start us, length us, event | category | flops | bytes accessed | tf_op | source)
XLA Modules:
  0.0 49.0 jit_solution(10280270139119641719)
XLA Ops:
  0.6 0.0 copy-start
  0.6 0.9 %copy-done = bf16[64,2048]{1,0:T(8,128)(2,1)S(1)} copy-done((bf16[64,2048]{1,0:T(8,128)(2,1)S(1)}, bf16[64,2048]{1,0:T(8,128)(2,1)}, u32[]{:S(2)}) %copy-start) | copy-done | bytes 262168
  1.6 0.0 copy-start.1
  1.6 0.9 %copy-done.1 = bf16[64,2048]{1,0:T(8,128)(2,1)S(1)} copy-done((bf16[64,2048]{1,0:T(8,128)(2,1)S(1)}, bf16[64,2048]{1,0:T(8,128)(2,1)}, u32[]{:S(2)}) %copy-start.1) | copy-done | bytes 262168
  2.5 0.0 copy-start.2
  2.5 0.7 %copy-done.2 = f32[2048]{0:T(1024)S(1)} copy-done((f32[2048]{0:T(1024)S(1)}, f32[2048]{0:T(1024)}, u32[]{:S(2)}) %copy-start.2) | copy-done | bytes 8216
  3.2 0.0 copy-start.3
  3.2 0.7 %copy-done.3 = f32[128]{0:T(128)S(1)} copy-done((f32[128]{0:T(128)S(1)}, f32[128]{0:T(128)}, u32[]{:S(2)}) %copy-start.3) | copy-done | bytes 536
  3.9 0.0 copy-start.4
  3.9 0.7 %copy-done.4 = f32[64]{0:T(128)S(1)} copy-done((f32[64]{0:T(128)S(1)}, f32[64]{0:T(128)}, u32[]{:S(2)}) %copy-start.4) | copy-done | bytes 280
  4.5 0.0 copy-start.5
  4.5 0.7 %copy-done.5 = f32[64]{0:T(128)S(1)} copy-done((f32[64]{0:T(128)S(1)}, f32[64]{0:T(128)}, u32[]{:S(2)}) %copy-start.5) | copy-done | bytes 280
  5.2 0.0 copy-start.6
  5.2 1.6 %copy-done.6 = bf16[1024,1024]{1,0:T(8,128)(2,1)S(1)} copy-done((bf16[1024,1024]{1,0:T(8,128)(2,1)S(1)}, bf16[1024,1024]{1,0:T(8,128)(2,1)}, u32[]{:S(2)}) %copy-start.6) | copy-done | bytes 2097176
  6.8 0.0 copy-start.7
  6.8 1.0 %copy-done.7 = f32[512,256]{1,0:T(8,128)S(1)} copy-done((f32[512,256]{1,0:T(8,128)S(1)}, f32[512,256]{1,0:T(8,128)}, u32[]{:S(2)}) %copy-start.7) | copy-done | bytes 524312
  7.8 0.0 copy-start.8
  7.8 1.0 %copy-done.8 = bf16[768,256]{1,0:T(8,128)(2,1)S(1)} copy-done((bf16[768,256]{1,0:T(8,128)(2,1)S(1)}, bf16[768,256]{1,0:T(8,128)(2,1)}, u32[]{:S(2)}) %copy-start.8) | copy-done | bytes 393240
  8.8 0.0 copy-start.9
  8.8 1.0 %copy-done.9 = bf16[768,256]{1,0:T(8,128)(2,1)S(1)} copy-done((bf16[768,256]{1,0:T(8,128)(2,1)S(1)}, bf16[768,256]{1,0:T(8,128)(2,1)}, u32[]{:S(2)}) %copy-start.9) | copy-done | bytes 393240
  9.8 37.4 %shard_map.130 = (bf16[64,2048]{1,0:T(8,128)(2,1)S(1)}, f32[4,128]{1,0:T(4,128)S(1)}, f32[1,128]{1,0:T(1,128)S(1)}) custom-call(bf16[64,2048]{1,0:T(8,128)(2,1)S(1)} %copy-done, bf16[64,2048]{1,0:T(8,128)(2,1)S(1)} %copy-done.1, f32[16,128]{1,0:T(8,128)S(1)} %bitcast.5, f32[1,128]{1,0:T(1,128)S(1)} %bitcast.6, f32[64]{0:T(128)S(1)} %copy-done.4, ...), custom_call_target="tpu_custom_call" | custom-call | flops 6000000000 | bytes 8000000 | tf_op jit(solution)/shard_map/pallas_call | solution.py:365
  47.3 0.7 %copy.17 = bf16[64,2048]{1,0:T(8,128)(2,1)} copy(bf16[64,2048]{1,0:T(8,128)(2,1)S(1)} %get-tuple-element.12) | data formatting | bytes 524288
  48.0 0.6 %copy.18 = f32[512]{0:T(512)} copy(f32[512]{0:T(512)S(1)} %bitcast.4) | data formatting | bytes 4096
  48.5 0.5 %copy.19 = f32[128]{0:T(128)} copy(f32[128]{0:T(128)S(1)} %bitcast.7) | data formatting | bytes 1024
Async XLA Ops:
  0.6 1.0 %copy-start = (bf16[64,2048]{1,0:T(8,128)(2,1)S(1)}, bf16[64,2048]{1,0:T(8,128)(2,1)}, u32[]{:S(2)}) copy-start(bf16[64,2048]{1,0:T(8,128)(2,1)} %refs_0_.1) | copy-start | bytes 786436
  1.6 0.9 %copy-start.1 = (bf16[64,2048]{1,0:T(8,128)(2,1)S(1)}, bf16[64,2048]{1,0:T(8,128)(2,1)}, u32[]{:S(2)}) copy-start(bf16[64,2048]{1,0:T(8,128)(2,1)} %refs_1_.1) | copy-start | bytes 786436
  2.5 0.7 %copy-start.2 = (f32[2048]{0:T(1024)S(1)}, f32[2048]{0:T(1024)}, u32[]{:S(2)}) copy-start(f32[2048]{0:T(1024)} %param.13) | copy-start | bytes 24580
  3.2 0.7 %copy-start.3 = (f32[128]{0:T(128)S(1)}, f32[128]{0:T(128)}, u32[]{:S(2)}) copy-start(f32[128]{0:T(128)} %param.14) | copy-start | bytes 1540
  3.9 0.7 %copy-start.4 = (f32[64]{0:T(128)S(1)}, f32[64]{0:T(128)}, u32[]{:S(2)}) copy-start(f32[64]{0:T(128)} %refs_4_.1) | copy-start | bytes 772
  4.5 0.7 %copy-start.5 = (f32[64]{0:T(128)S(1)}, f32[64]{0:T(128)}, u32[]{:S(2)}) copy-start(f32[64]{0:T(128)} %refs_5_.1) | copy-start | bytes 772
  5.2 1.6 %copy-start.6 = (bf16[1024,1024]{1,0:T(8,128)(2,1)S(1)}, bf16[1024,1024]{1,0:T(8,128)(2,1)}, u32[]{:S(2)}) copy-start(bf16[1024,1024]{1,0:T(8,128)(2,1)} %constant.10.clone.refs_6_) | copy-start | bytes 6291460
  6.8 1.0 %copy-start.7 = (f32[512,256]{1,0:T(8,128)S(1)}, f32[512,256]{1,0:T(8,128)}, u32[]{:S(2)}) copy-start(f32[512,256]{1,0:T(8,128)} %constant.12.clone.refs_8_) | copy-start | bytes 1572868
  7.8 1.0 %copy-start.8 = (bf16[768,256]{1,0:T(8,128)(2,1)S(1)}, bf16[768,256]{1,0:T(8,128)(2,1)}, u32[]{:S(2)}) copy-start(bf16[768,256]{1,0:T(8,128)(2,1)} %constant.14.clone.refs_10_) | copy-start | bytes 1179652
  8.8 1.0 %copy-start.9 = (bf16[768,256]{1,0:T(8,128)(2,1)S(1)}, bf16[768,256]{1,0:T(8,128)(2,1)}, u32[]{:S(2)}) copy-start(bf16[768,256]{1,0:T(8,128)(2,1)} %constant.13.clone.refs_9_) | copy-start | bytes 1179652

commit v2 on v1

v2 whole, which is shorter than its diff:
```python
import math

import jax
import jax.numpy as jnp
import ml_dtypes
import numpy as np
from jax import lax
from jax.experimental import pallas as pl
from jax.experimental.pallas import tpu as pltpu
from jax.sharding import PartitionSpec as P

MESH = pl.DeviceIdType.MESH
F32, BF16 = jnp.float32, jnp.bfloat16
N1, N2 = 512, 128
LEN = N1 * N2
HALF = N1 // 2


def split_np(x):
    x = x.astype(np.float32)
    hi = x.astype(ml_dtypes.bfloat16)
    lo = (x - hi.astype(np.float32)).astype(ml_dtypes.bfloat16)
    return hi, lo


def tables():
    k = np.arange(N1, dtype=np.float64)[:, None] + 0.25
    kh = k[:HALF]
    fwd, inv = [], []
    for odd in range(2):
        n = 2 * np.arange(HALF, dtype=np.float64)[None, :] + odd
        ang = -2 * np.pi * np.mod(kh * n, N1) / N1
        hi, lo = split_np(np.concatenate([np.cos(ang), np.sin(ang)], axis=0))
        fwd.append(np.concatenate([hi, lo], axis=1))
        inv.append(np.concatenate([hi.T, lo.T], axis=1))
    m = np.arange(N2, dtype=np.float64)
    ang = -2 * np.pi * k * m[None, :] / LEN
    twist = np.concatenate([np.cos(ang), np.sin(ang)], axis=1).astype(np.float32)
    ang = -2 * np.pi * np.mod(m[:, None] * m[None, :], N2) / N2
    br, bi = np.cos(ang), np.sin(ang)
    b_hi, b_lo = split_np(np.block([[br, bi], [-bi, br]]))
    c_hi, c_lo = split_np(np.block([[br, -bi], [bi, br]]) / LEN)
    mix = np.concatenate([b_hi, b_hi, b_lo, c_hi, c_hi, c_lo])
    return np.concatenate(fwd), np.concatenate(inv), twist, mix


def dot(a, b):
    return jnp.dot(a, b, preferred_element_type=F32)


def split(x):
    hi = x.astype(BF16)
    return hi, (x - hi.astype(F32)).astype(BF16)


def split3(x):
    hi, lo = split(x)
    return jnp.concatenate([hi, lo, hi], axis=1)


def twice(x):
    return jnp.concatenate([x, x], axis=0)


def mix_forward(even, odd, twist, mix, z_refs):
    for q, z in enumerate(z_refs):
        s = slice(q * N2, (q + 1) * N2)
        er, ei, dr, di = even[:HALF, s], even[HALF:, s], odd[:HALF, s], odd[HALF:, s]
        for h, (xr, xi) in enumerate([(er + dr, ei + di), (er - dr, ei - di)]):
            r = slice(h * HALF, (h + 1) * HALF)
            tr, ti = twist[r, :N2], twist[r, N2:]
            y = jnp.concatenate([xr * tr - xi * ti, xi * tr + xr * ti], axis=1)
            z[r, :] = dot(split3(y), mix[:768, :])


def forward_exact(xe, xo, fwd, twist, mix, z_refs):
    mix_forward(dot(fwd[:N1, :], twice(xe)), dot(fwd[N1:, :], twice(xo)), twist, mix, z_refs)


def forward_split(xe, xo, fwd, twist, mix, z_refs):
    out = []
    for h, x in enumerate((xe, xo)):
        hi, lo = split(x)
        r = slice(h * N1, (h + 1) * N1)
        out.append(dot(fwd[r, :], twice(hi)) + dot(fwd[r, :HALF], lo))
    mix_forward(out[0], out[1], twist, mix, z_refs)


def inverse_pair(left, right, inv, twist, mix):
    plus, minus = [], []
    for a, b in zip(left, right):
        ys = []
        for h in range(2):
            r = slice(h * HALF, (h + 1) * HALF)
            ar, ai, br, bi = a[r, :N2], a[r, N2:], b[r, :N2], b[r, N2:]
            z = jnp.concatenate([ar * br + ai * bi, ai * br - ar * bi], axis=1)
            y = dot(split3(z), mix[768:, :])
            yr, yi = y[:, :N2], y[:, N2:]
            tr, ti = twist[r, :N2], twist[r, N2:]
            ys.append(jnp.concatenate([yr * tr + yi * ti, yi * tr - yr * ti], axis=0))
        plus.append(ys[0] + ys[1])
        minus.append(ys[0] - ys[1])
    out = []
    for h, y in enumerate((plus, minus)):
        hi, lo = split(jnp.concatenate(y, axis=1))
        r = slice(h * HALF, (h + 1) * HALF)
        out.append(dot(inv[r, :], twice(hi)) + dot(inv[r, :N1], lo))
    return out


def dot3(a, b):
    ah, al = split(a)
    bh, bl = split(b)
    return dot(ah, bh) + (dot(ah, bl) + dot(al, bh))


def dot3_nt(a, b):
    def nt(x, y):
        return lax.dot_general(x, y, (((1,), (1,)), ((), ())), preferred_element_type=F32)

    ah, al = split(a)
    bh, bl = split(b)
    return nt(ah, bh) + (nt(ah, bl) + nt(al, bh))


def one_hot(cond):
    return jnp.where(cond, 1.0, 0.0).astype(BF16)


def swap_matrix(back):
    i = lax.broadcasted_iota(jnp.int32, (256, 256), 0)
    j = lax.broadcasted_iota(jnp.int32, (256, 256), 1)
    if back:
        i, j = j, i
    p = i % 16
    return one_hot((i // 16 == j % 16) & (2 * (p % 8) + p // 8 == j // 16))


def long_and_short(r_buf, even, odd, f_buf, w_row, alpha, lam):
    re, ro = even[:, :N2] + even[:, N2:], odd[:, :N2] + odd[:, N2:]
    r_buf[:HALF, :] = re
    pair = jnp.concatenate(
        [jnp.concatenate([re, ro], axis=1), jnp.concatenate([ro, r_buf[pl.ds(1, HALF), :]], axis=1)], axis=0
    )
    zero = jnp.zeros((1, N2), F32)
    base = jnp.broadcast_to(jnp.concatenate([w_row, zero], axis=1), (N2, 2 * N2))
    toep = pltpu.roll(base, 0, 1, stride=1, stride_axis=0)
    long = dot3_nt(pair, toep)
    long_e = long[:HALF] + (alpha[0] * even[:, :N2] + alpha[1] * even[:, N2:])
    long_o = long[HALF:] + (alpha[0] * odd[:, :N2] + alpha[1] * odd[:, N2:])
    f = jnp.concatenate([f_buf[0, 8:, :], f_buf[1, 8:, :]], axis=0)
    cross = dot3(jnp.transpose(f), pair)
    i = lax.broadcasted_iota(jnp.int32, (N2, N2), 0)
    j = lax.broadcasted_iota(jnp.int32, (N2, N2), 1)
    flip = one_hot(i + j == N2 - 1)
    ch, cl = split(cross)
    diag = pltpu.roll(dot(flip, ch) + dot(flip, cl), N2 + 1, 1, stride=1, stride_axis=0)
    short = jnp.sum(diag, axis=0, keepdims=True)[:, :N2]
    return long_e, long_o, short + (lam[0] * even[:1, :N2] + lam[1] * even[:1, N2:])


def filters(f_buf, w_row, alpha, lam):
    fe, fo = f_buf[0, 8:, :], f_buf[1, 8:, :]
    pair = jnp.concatenate(
        [
            jnp.concatenate([f_buf[1, pl.ds(7, HALF), :], fe], axis=1),
            jnp.concatenate([fe, fo], axis=1),
        ],
        axis=0,
    )
    zero = jnp.zeros((1, N2), F32)
    base = jnp.broadcast_to(jnp.concatenate([zero, w_row], axis=1), (2 * N2, 2 * N2))
    toep = pltpu.roll(base, 0, 1, stride=1, stride_axis=0)[:, :N2]
    u = dot3(pair, toep)
    first_row = lax.broadcasted_iota(jnp.int32, (8, N2), 0) == 0
    first = first_row & (lax.broadcasted_iota(jnp.int32, (8, N2), 1) == 0)
    ve, vo = [], []
    for c in range(2):
        v = u[:HALF] + alpha[c] * fe
        extra = jnp.where(first_row, lam[c] * w_row, 0.0) + jnp.where(first, lam[c] * alpha[c], 0.0)
        ve.append(jnp.concatenate([v[:8] + extra, v[8:]], axis=0))
        vo.append(u[HALF:] + alpha[c] * fo)
    return jnp.concatenate(ve, axis=1), jnp.concatenate(vo, axis=1)


def halves(x):
    x = x.astype(F32).reshape(32, 16, N2)
    return x[:, :8].reshape(HALF, N2).astype(BF16), x[:, 8:].reshape(HALF, N2).astype(BF16)


def offsets():
    def far(o):
        return o[0] + min(o[1], 4 - o[1]) + min(o[2], 4 - o[2])

    out = [(y, z, x) for y in range(2) for z in range(4) for x in range(4)][1:]
    return sorted(out, key=lambda o: -far(o))


def kernel(
    n_ctx, n_tp,
    sig, cot, filt, w_in, lam_in, alpha_in, f_tab, i_tab, t_tab, m_tab,
    sg_recv, t_recv,
    sig_v, cot_v, filt_v, filt_s, w_v, lam_s, alpha_s, fwd, inv, twist, mix,
    send, recv, f_buf, zs0, zg0, zs1, zg1, zv0, zv1, r_buf, l_send, l_recv, t_send, sg_send,
    load_sem, send_sem, recv_sem,
):
    me, tp = lax.axis_index("ctx"), lax.axis_index("tp")
    my_y, my_z, my_x = me // 16, (me // 4) % 4, me % 4
    peers = [((my_y + y) % 2) * 16 + ((my_z + z) % 4) * 4 + (my_x + x) % 4 for y, z, x in offsets()]
    tp_peers = [(tp + i) % n_tp for i in (2, 3, 1)]
    n_peers = len(peers)

    barrier = pltpu.get_barrier_semaphore()
    loads = [
        pltpu.make_async_copy(src, dst, load_sem.at[i])
        for i, (src, dst) in enumerate(
            [(filt, filt_v), (sig, sig_v), (cot, cot_v), (w_in, w_v), (lam_in, lam_s), (alpha_in, alpha_s),
             (f_tab, fwd), (t_tab, twist), (m_tab, mix), (i_tab, inv)]
        )
    ]
    for c in loads:
        c.start()
    for e in peers:
        pl.semaphore_signal(barrier, inc=1, device_id={"ctx": e}, device_id_type=MESH)
    for t in tp_peers:
        pl.semaphore_signal(barrier, inc=1, device_id={"tp": t}, device_id_type=MESH)
    f_buf[:, :8, :] = jnp.zeros((2, 8, N2), F32)
    r_buf[HALF:, :] = jnp.zeros((8, N2), F32)
    swap = swap_matrix(False)
    for c in loads[:3]:
        c.wait()
    for h in range(2):
        for i in range(8):
            filt_s[h, i : i + 1, :] = filt_v[2 * i + h : 2 * i + h + 1, :]
    for g in range(4):
        ch = slice(16 * g, 16 * (g + 1))
        x = jnp.concatenate(
            [
                jnp.concatenate([v[ch, N2 * a : N2 * (a + 1)] for a in range(16)], axis=0)
                for v in (sig_v, cot_v)
            ],
            axis=1,
        )
        y = dot(swap, x).astype(BF16)
        send[ch, 0] = y[:, :N2].reshape(16, 16, N2)
        send[ch, 1] = y[:, N2:].reshape(16, 16, N2)
    pl.semaphore_wait(barrier, n_peers + len(tp_peers))

    rows_me = pl.ds(pl.multiple_of(16 * me, 16), 16)
    f_dst = f_buf.at[:, pl.ds(pl.multiple_of(8 + 8 * me, 8), 8), :]

    def remote(src, dst, k, where):
        pltpu.make_async_remote_copy(
            src_ref=src, dst_ref=dst, send_sem=send_sem.at[k], recv_sem=recv_sem.at[k],
            device_id=where, device_id_type=MESH,
        ).start()

    def local(src, dst, k):
        pltpu.make_async_copy(src, dst, recv_sem.at[k]).start()

    def finish(ref, sem):
        pltpu.make_async_copy(ref, ref, sem).wait()

    for e in peers:
        remote(filt_s, f_dst, 0, {"ctx": e})
    for c in range(2):
        for e in peers:
            remote(send.at[2 * e + c], recv.at[c, :, rows_me, :], 1 + c, {"ctx": e})
    local(filt_s, f_dst, 0)
    for c in range(2):
        local(send.at[2 * me + c], recv.at[c, :, rows_me, :], 1 + c)

    for c in loads[3:]:
        c.wait()
    w_row = w_v[...]
    alpha = (alpha_s[2 * me], alpha_s[2 * me + 1])
    lam = (lam_s[2 * me], lam_s[2 * me + 1])

    finish(f_buf.at[:, pl.ds(8, HALF), :], recv_sem.at[0])
    ve, vo = filters(f_buf, w_row, alpha, lam)
    forward_split(ve, vo, fwd, twist, mix, (zv0, zv1))
    for c, zs in enumerate(((zs0, zg0), (zs1, zg1))):
        finish(recv.at[c], recv_sem.at[1 + c])
        se, so = halves(recv[c, 0])
        ge, go = halves(recv[c, 1])
        forward_exact(
            jnp.concatenate([se, ge], axis=1), jnp.concatenate([so, go], axis=1), fwd, twist, mix, zs
        )
    even, odd = inverse_pair((zg0, zg1), (zs0, zs1), inv, twist, mix)
    long_e, long_o, short = long_and_short(r_buf, even, odd, f_buf, w_row, alpha, lam)
    l_send[:, :8, :] = long_e.reshape(32, 8, N2)
    l_send[:, 8:16, :] = long_o.reshape(32, 8, N2)
    l_send[:, 16:, :] = jnp.broadcast_to(short.reshape(1, 1, N2), (32, 8, N2))
    for e in peers:
        remote(l_send.at[e], l_recv.at[me], 3, {"ctx": e})
    local(l_send.at[me], l_recv.at[me], 3)

    even, odd = inverse_pair((zg0, zg1), (zv0, zv1), inv, twist, mix)
    for c in range(2):
        s = slice(c * N2, (c + 1) * N2)
        rows = jnp.concatenate([even[:, s].reshape(32, 8, N2), odd[:, s].reshape(32, 8, N2)], axis=1)
        sg_send[c] = rows.astype(BF16)
    sg_dst = sg_recv.at[pl.ds(2 * me, 2)]
    for e in peers:
        remote(sg_send.at[:, e], sg_dst, 4, {"ctx": e})
    local(sg_send.at[:, me], sg_dst, 4)

    finish(l_recv, recv_sem.at[3])
    total = l_recv[0]
    for d in range(1, 32):
        total = total + l_recv[d]
    for t in range(4):
        for i in range(4):
            r = 8 * (i % 2) + 2 * t + i // 2
            t_send[t, i : i + 1, :] = total[r : r + 1]
        t_send[t, 4:, :] = total[16:20]
    for t in tp_peers:
        remote(t_send.at[t], t_recv.at[tp], 5, {"tp": t})
    local(t_send.at[tp], t_recv.at[tp], 5)

    finish(sg_recv, recv_sem.at[4])
    finish(t_recv, recv_sem.at[5])
    finish(f_buf.at[:, pl.ds(8, 8 * n_peers), :], send_sem.at[0])
    finish(send.at[pl.ds(0, n_peers)], send_sem.at[1])
    finish(send.at[pl.ds(0, n_peers)], send_sem.at[2])
    finish(l_send.at[pl.ds(0, n_peers)], send_sem.at[3])
    finish(sg_send.at[:, pl.ds(0, n_peers)], send_sem.at[4])
    finish(t_send.at[pl.ds(0, 3)], send_sem.at[5])


def lay_out(sg_in, t_in, sg_out, long_out, short_out):
    swap = swap_matrix(True)
    for g in range(2):
        x = jnp.concatenate(
            [sg_in[32 * g + 16 * h : 32 * g + 16 * (h + 1)].reshape(256, N2) for h in range(2)], axis=1
        )
        y = dot(swap, x).astype(BF16)
        for h in range(2):
            ch = slice(32 * g + 16 * h, 32 * g + 16 * (h + 1))
            for a in range(16):
                sg_out[ch, N2 * a : N2 * (a + 1)] = y[16 * a : 16 * (a + 1), h * N2 : (h + 1) * N2]
    whole = (t_in[0] + t_in[1]) + (t_in[2] + t_in[3])
    long_out[...] = whole[:4]
    short_out[...] = whole[4:5]


def shards(signal, grad_out, long_filter, short_filter, long_skip, short_skip):
    n_ctx, n_tp = lax.axis_size("ctx"), lax.axis_size("tp")
    consts = [jnp.asarray(t) for t in tables()]
    hbm = pl.BlockSpec(memory_space=pltpu.HBM)
    vmem = pl.BlockSpec(memory_space=pltpu.VMEM)
    V, S = pltpu.VMEM, pltpu.SMEM
    spec = V((N1, 2 * N2), F32)
    raw_sg, raw_t = pl.pallas_call(
        lambda *refs: kernel(n_ctx, n_tp, *refs),
        out_shape=(
            jax.ShapeDtypeStruct((64, 16, N2), BF16),
            jax.ShapeDtypeStruct((4, 8, N2), F32),
        ),
        in_specs=[hbm] * 10,
        out_specs=(vmem, vmem),
        scratch_shapes=[
            V((64, 2048), BF16), V((64, 2048), BF16), V((16, N2), F32), V((2, 8, N2), F32),
            V((1, N2), F32), S((64,), F32), S((64,), F32),
            V((2 * N1, N1), BF16), V((N1, 2 * N1), BF16), V((N1, 2 * N2), F32), V((1536, 256), BF16),
            V((64, 2, 16, N2), BF16), V((2, 2, N1, N2), BF16), V((2, HALF + 8, N2), F32),
            spec, spec, spec, spec, spec, spec, V((HALF + 8, N2), F32),
            V((32, 24, N2), F32), V((32, 24, N2), F32), V((4, 8, N2), F32), V((2, 32, 16, N2), BF16),
            pltpu.SemaphoreType.DMA((10,)), pltpu.SemaphoreType.DMA((6,)), pltpu.SemaphoreType.DMA((6,)),
        ],
        compiler_params=pltpu.CompilerParams(
            collective_id=0, has_side_effects=True, vmem_limit_bytes=60 * 1024 * 1024
        ),
        cost_estimate=pl.CostEstimate(flops=6_000_000_000, bytes_accessed=8_000_000, transcendentals=0),
    )(
        signal, grad_out, long_filter.reshape(16, N2), short_filter.reshape(1, N2),
        long_skip, short_skip, *consts,
    )
    sg, long, short = pl.pallas_call(
        lay_out,
        out_shape=(
            jax.ShapeDtypeStruct((64, 2048), BF16),
            jax.ShapeDtypeStruct((4, N2), F32),
            jax.ShapeDtypeStruct((1, N2), F32),
        ),
        in_specs=[vmem, vmem],
        out_specs=(vmem, vmem, vmem),
    )(raw_sg, raw_t)
    return sg, long.reshape(512), short.reshape(N2)


def solution(mesh):
    placed = (P("tp", "ctx"), P("tp", "ctx"), P("ctx"), P(), P("tp"), P("tp"))
    return jax.shard_map(
        shards,
        mesh=mesh,
        in_specs=placed,
        out_specs=(P("tp", "ctx"), P(("ctx", "tp")), P()),
        check_vma=False,
    )
```

time: 50 us -> 38 us (0.76); the launches traced: 49 us -> 37.9 us
  local copies, waits for them, and re-layouts: 11 us -> 0 us
    unnamed x23 -> x0, local copies, waits for them, and re-layouts: 11 us -> none
    pallas_call x1, Pallas kernels: 37.4 us -> 35.4 us  [shards(): pl.pallas_call(lambda *refs: kernel(n_ctx, n_tp, *refs), out_shape=(jax.S...]
    pallas_call x0 -> x1, Pallas kernels: none -> 1.9 us  [shards(): pl.pallas_call(lay_out, out_shape=(jax.ShapeDtypeStruct((64, 2048), BF16)...]
where the time goes in v2:
time: 38 us; the launch traced here: 37.9 us
  Pallas kernels  37.3 us (98%)
  between operations  0.64 us (2%)
    pallas_call x1, Pallas kernels, shards(): pl.pallas_call(lambda *refs: kernel(n_ctx, n_tp, *refs), out_shape=(jax.S...  35.4 us
    pallas_call x1, Pallas kernels, shards(): pl.pallas_call(lay_out, out_shape=(jax.ShapeDtypeStruct((64, 2048), BF16)...  1.9 us

profile of v2, /device:TPU:1, one launch (start us, length us, event | category | flops | bytes accessed | tf_op | source)
XLA Modules:
  0.0 37.9 jit_solution(5866037300533956144)
XLA Ops:
  0.6 35.4 %shard_map.121 = (bf16[64,16,128]{2,1,0:T(8,128)(2,1)}, f32[4,8,128]{2,1,0:T(8,128)}) custom-call(bf16[64,2048]{1,0:T(8,128)(2,1)} %refs_0_.1, bf16[64,2048]{1,0:T(8,128)(2,1)} %refs_1_.1, f32[16,128]{1,0:T(8,128)} %bitcast.4, f32[1,128]{1,0:T(1,128)} %bitcast.6, f32[64]{0:T(128)} %refs_4_.1, f32[64]{0:T(128)} %refs_5_.1, ...), custom_call_target="tpu_custom_call" | custom-call | flops 6000000000 | bytes 8000000 | tf_op jit(solution)/shard_map/pallas_call | solution.py:354
  36.0 1.9 %shard_map.122 = (bf16[64,2048]{1,0:T(8,128)(2,1)}, f32[4,128]{1,0:T(4,128)}, f32[1,128]{1,0:T(1,128)}) custom-call(bf16[64,16,128]{2,1,0:T(8,128)(2,1)} %get-tuple-element.8.sg_in, f32[4,8,128]{2,1,0:T(8,128)} %get-tuple-element.9.t_in), custom_call_target="tpu_custom_call" | custom-call | tf_op jit(solution)/shard_map/pallas_call | solution.py:379

commit v3 on v2

--- a/solution.py
+++ b/solution.py
@@ -108,21 +108,6 @@
     return out
 
 
-def dot3(a, b):
-    ah, al = split(a)
-    bh, bl = split(b)
-    return dot(ah, bh) + (dot(ah, bl) + dot(al, bh))
-
-
-def dot3_nt(a, b):
-    def nt(x, y):
-        return lax.dot_general(x, y, (((1,), (1,)), ((), ())), preferred_element_type=F32)
-
-    ah, al = split(a)
-    bh, bl = split(b)
-    return nt(ah, bh) + (nt(ah, bl) + nt(al, bh))
-
-
 def one_hot(cond):
     return jnp.where(cond, 1.0, 0.0).astype(BF16)
 
@@ -136,30 +121,43 @@
     return one_hot((i // 16 == j % 16) & (2 * (p % 8) + p // 8 == j // 16))
 
 
-def long_and_short(r_buf, even, odd, f_buf, w_row, alpha, lam):
-    re, ro = even[:, :N2] + even[:, N2:], odd[:, :N2] + odd[:, N2:]
-    r_buf[:HALF, :] = re
+def rolled(w_row, first, rows):
+    zero = jnp.zeros((1, N2), F32)
+    base = jnp.concatenate([w_row, zero] if first else [zero, w_row], axis=1)
+    return pltpu.roll(jnp.broadcast_to(base, (rows, 2 * N2)), 0, 1, stride=1, stride_axis=0)
+
+
+def stack3(x):
+    hi, lo = split(x)
+    return jnp.concatenate([hi, hi, lo], axis=0)
+
+
+def long_rows(re, ro, r_buf, band, alpha):
+    se, so = re[0] + re[1], ro[0] + ro[1]
+    r_buf[:HALF, :] = se
     pair = jnp.concatenate(
-        [jnp.concatenate([re, ro], axis=1), jnp.concatenate([ro, r_buf[pl.ds(1, HALF), :]], axis=1)], axis=0
+        [jnp.concatenate([se, so], axis=1), jnp.concatenate([so, r_buf[pl.ds(1, HALF), :]], axis=1)], axis=0
     )
-    zero = jnp.zeros((1, N2), F32)
-    base = jnp.broadcast_to(jnp.concatenate([w_row, zero], axis=1), (N2, 2 * N2))
-    toep = pltpu.roll(base, 0, 1, stride=1, stride_axis=0)
-    long = dot3_nt(pair, toep)
-    long_e = long[:HALF] + (alpha[0] * even[:, :N2] + alpha[1] * even[:, N2:])
-    long_o = long[HALF:] + (alpha[0] * odd[:, :N2] + alpha[1] * odd[:, N2:])
-    f = jnp.concatenate([f_buf[0, 8:, :], f_buf[1, 8:, :]], axis=0)
-    cross = dot3(jnp.transpose(f), pair)
+    long = dot(split3(pair), band)
+    long_e = long[:HALF] + (alpha[0] * re[0] + alpha[1] * re[1])
+    long_o = long[HALF:] + (alpha[0] * ro[0] + alpha[1] * ro[1])
+    return long_e, long_o, pair
+
+
+def short_row(pair, f_t, re, lam):
+    th, tl = split(f_t)
+    ph, plo = split(pair)
+    cross = dot(th, ph) + (dot(th, plo) + dot(tl, ph))
     i = lax.broadcasted_iota(jnp.int32, (N2, N2), 0)
     j = lax.broadcasted_iota(jnp.int32, (N2, N2), 1)
     flip = one_hot(i + j == N2 - 1)
     ch, cl = split(cross)
     diag = pltpu.roll(dot(flip, ch) + dot(flip, cl), N2 + 1, 1, stride=1, stride_axis=0)
     short = jnp.sum(diag, axis=0, keepdims=True)[:, :N2]
-    return long_e, long_o, short + (lam[0] * even[:1, :N2] + lam[1] * even[:1, N2:])
-
-
-def filters(f_buf, w_row, alpha, lam):
+    return short + (lam[0] * re[0][:1, :] + lam[1] * re[1][:1, :])
+
+
+def filters(f_buf, w_row, band, alpha, lam):
     fe, fo = f_buf[0, 8:, :], f_buf[1, 8:, :]
     pair = jnp.concatenate(
         [
@@ -168,10 +166,7 @@
         ],
         axis=0,
     )
-    zero = jnp.zeros((1, N2), F32)
-    base = jnp.broadcast_to(jnp.concatenate([zero, w_row], axis=1), (2 * N2, 2 * N2))
-    toep = pltpu.roll(base, 0, 1, stride=1, stride_axis=0)[:, :N2]
-    u = dot3(pair, toep)
+    u = dot(split3(pair), band)
     first_row = lax.broadcasted_iota(jnp.int32, (8, N2), 0) == 0
     first = first_row & (lax.broadcasted_iota(jnp.int32, (8, N2), 1) == 0)
     ve, vo = [], []
@@ -199,16 +194,19 @@
 def kernel(
     n_ctx, n_tp,
     sig, cot, filt, w_in, lam_in, alpha_in, f_tab, i_tab, t_tab, m_tab,
-    sg_recv, t_recv,
+    sg_recv, long_out, short_out,
     sig_v, cot_v, filt_v, filt_s, w_v, lam_s, alpha_s, fwd, inv, twist, mix,
-    send, recv, f_buf, zs0, zg0, zs1, zg1, zv0, zv1, r_buf, l_send, l_recv, t_send, sg_send,
-    load_sem, send_sem, recv_sem,
+    send, recv, f_buf, zs, zg, zv0, zv1, r_buf, band_a, band_c, f_t,
+    l_send, l_recv, s_send, s_recv, sg_send, load_sem, send_sem, recv_sem, ready,
 ):
     me, tp = lax.axis_index("ctx"), lax.axis_index("tp")
+    zv = (zv0, zv1)
     my_y, my_z, my_x = me // 16, (me // 4) % 4, me % 4
     peers = [((my_y + y) % 2) * 16 + ((my_z + z) % 4) * 4 + (my_x + x) % 4 for y, z, x in offsets()]
     tp_peers = [(tp + i) % n_tp for i in (2, 3, 1)]
     n_peers = len(peers)
+    n_all = n_ctx * n_tp
+    my_id = n_tp * me + tp
 
     barrier = pltpu.get_barrier_semaphore()
     loads = [
@@ -227,7 +225,7 @@
     f_buf[:, :8, :] = jnp.zeros((2, 8, N2), F32)
     r_buf[HALF:, :] = jnp.zeros((8, N2), F32)
     swap = swap_matrix(False)
-    for c in loads[:3]:
+    for c in loads[:6]:
         c.wait()
     for h in range(2):
         for i in range(8):
@@ -244,7 +242,14 @@
         y = dot(swap, x).astype(BF16)
         send[ch, 0] = y[:, :N2].reshape(16, 16, N2)
         send[ch, 1] = y[:, N2:].reshape(16, 16, N2)
+    w_row = w_v[...]
+    band_a[...] = stack3(jnp.transpose(rolled(w_row, True, N2)))
+    band_c[...] = stack3(rolled(w_row, False, 2 * N2)[:, :N2])
+    alpha = (alpha_s[2 * me], alpha_s[2 * me + 1])
+    lam = (lam_s[2 * me], lam_s[2 * me + 1])
     pl.semaphore_wait(barrier, n_peers + len(tp_peers))
+    for t in tp_peers:
+        pl.semaphore_signal(ready, inc=1, device_id={"tp": t}, device_id_type=MESH)
 
     rows_me = pl.ds(pl.multiple_of(16 * me, 16), 16)
     f_dst = f_buf.at[:, pl.ds(pl.multiple_of(8 + 8 * me, 8), 8), :]
@@ -270,65 +275,64 @@
     for c in range(2):
         local(send.at[2 * me + c], recv.at[c, :, rows_me, :], 1 + c)
 
-    for c in loads[3:]:
+    for c in loads[6:]:
         c.wait()
-    w_row = w_v[...]
-    alpha = (alpha_s[2 * me], alpha_s[2 * me + 1])
-    lam = (lam_s[2 * me], lam_s[2 * me + 1])
-
     finish(f_buf.at[:, pl.ds(8, HALF), :], recv_sem.at[0])
-    ve, vo = filters(f_buf, w_row, alpha, lam)
-    forward_split(ve, vo, fwd, twist, mix, (zv0, zv1))
-    for c, zs in enumerate(((zs0, zg0), (zs1, zg1))):
+    ve, vo = filters(f_buf, w_row, band_c[...], alpha, lam)
+    forward_split(ve, vo, fwd, twist, mix, zv)
+    f_t[...] = jnp.transpose(jnp.concatenate([f_buf[0, 8:, :], f_buf[1, 8:, :]], axis=0))
+
+    re, ro = [], []
+    for c in range(2):
         finish(recv.at[c], recv_sem.at[1 + c])
         se, so = halves(recv[c, 0])
         ge, go = halves(recv[c, 1])
         forward_exact(
-            jnp.concatenate([se, ge], axis=1), jnp.concatenate([so, go], axis=1), fwd, twist, mix, zs
+            jnp.concatenate([se, ge], axis=1), jnp.concatenate([so, go], axis=1), fwd, twist, mix, (zs, zg)
         )
-    even, odd = inverse_pair((zg0, zg1), (zs0, zs1), inv, twist, mix)
-    long_e, long_o, short = long_and_short(r_buf, even, odd, f_buf, w_row, alpha, lam)
-    l_send[:, :8, :] = long_e.reshape(32, 8, N2)
-    l_send[:, 8:16, :] = long_o.reshape(32, 8, N2)
-    l_send[:, 16:, :] = jnp.broadcast_to(short.reshape(1, 1, N2), (32, 8, N2))
-    for e in peers:
-        remote(l_send.at[e], l_recv.at[me], 3, {"ctx": e})
-    local(l_send.at[me], l_recv.at[me], 3)
-
-    even, odd = inverse_pair((zg0, zg1), (zv0, zv1), inv, twist, mix)
-    for c in range(2):
-        s = slice(c * N2, (c + 1) * N2)
-        rows = jnp.concatenate([even[:, s].reshape(32, 8, N2), odd[:, s].reshape(32, 8, N2)], axis=1)
-        sg_send[c] = rows.astype(BF16)
-    sg_dst = sg_recv.at[pl.ds(2 * me, 2)]
-    for e in peers:
-        remote(sg_send.at[:, e], sg_dst, 4, {"ctx": e})
-    local(sg_send.at[:, me], sg_dst, 4)
-
-    finish(l_recv, recv_sem.at[3])
-    total = l_recv[0]
-    for d in range(1, 32):
-        total = total + l_recv[d]
-    for t in range(4):
-        for i in range(4):
-            r = 8 * (i % 2) + 2 * t + i // 2
-            t_send[t, i : i + 1, :] = total[r : r + 1]
-        t_send[t, 4:, :] = total[16:20]
-    for t in tp_peers:
-        remote(t_send.at[t], t_recv.at[tp], 5, {"tp": t})
-    local(t_send.at[tp], t_recv.at[tp], 5)
-
-    finish(sg_recv, recv_sem.at[4])
-    finish(t_recv, recv_sem.at[5])
+        even, odd = inverse_pair((zg, zg), (zs, zv[c]), inv, twist, mix)
+        re.append(even[:, :N2])
+        ro.append(odd[:, :N2])
+        rows = [x[:, N2:].reshape(32, 8, N2) for x in (even, odd)]
+        sg_send[c] = jnp.concatenate(rows, axis=1).astype(BF16)
+        for e in peers:
+            remote(sg_send.at[c, e], sg_recv.at[2 * me + c], 3 + c, {"ctx": e})
+        local(sg_send.at[c, me], sg_recv.at[2 * me + c], 3 + c)
+
+    long_e, long_o, pair = long_rows(re, ro, r_buf, band_a[...], alpha)
+    l_send[pl.ds(0, HALF, 2), :] = long_e
+    l_send[pl.ds(1, HALF, 2), :] = long_o
+    pl.semaphore_wait(ready, len(tp_peers))
+    everyone = [(e, t) for t in tp_peers for e in peers] + [(me, t) for t in tp_peers] + [(e, tp) for e in peers]
+    l_dst = l_recv.at[pl.ds(pl.multiple_of(4 * my_id, 4), 4), :]
+    for e, t in everyone:
+        src = l_send.at[pl.ds(pl.multiple_of(4 * (n_tp * e + t), 4), 4), :]
+        remote(src, l_dst, 5, {"ctx": e, "tp": t})
+    local(l_send.at[pl.ds(pl.multiple_of(4 * my_id, 4), 4), :], l_dst, 5)
+
+    s_send[...] = short_row(pair, f_t[...], re, lam)
+    s_dst = s_recv.at[pl.ds(my_id, 1), :]
+    for e, t in everyone:
+        remote(s_send, s_dst, 6, {"ctx": e, "tp": t})
+    local(s_send, s_dst, 6)
+
+    finish(l_recv, recv_sem.at[5])
+    total = jnp.sum(l_recv[...].reshape(64, 8, N2), axis=0)
+    long_out[...] = total[:4] + total[4:]
+    finish(s_recv, recv_sem.at[6])
+    short_out[...] = jnp.sum(s_recv[...], axis=0, keepdims=True)
+    for c in range(2):
+        finish(sg_send.at[c], recv_sem.at[3 + c])
     finish(f_buf.at[:, pl.ds(8, 8 * n_peers), :], send_sem.at[0])
     finish(send.at[pl.ds(0, n_peers)], send_sem.at[1])
     finish(send.at[pl.ds(0, n_peers)], send_sem.at[2])
-    finish(l_send.at[pl.ds(0, n_peers)], send_sem.at[3])
-    finish(sg_send.at[:, pl.ds(0, n_peers)], send_sem.at[4])
-    finish(t_send.at[pl.ds(0, 3)], send_sem.at[5])
-
-
-def lay_out(sg_in, t_in, sg_out, long_out, short_out):
+    for c in range(2):
+        finish(sg_send.at[c, pl.ds(0, n_peers)], send_sem.at[3 + c])
+    finish(l_send.at[pl.ds(0, 4 * (n_all - 1)), :], send_sem.at[5])
+    finish(s_recv.at[pl.ds(0, n_all - 1), :], send_sem.at[6])
+
+
+def lay_out(sg_in, long_in, short_in, sg_out, long_out, short_out):
     swap = swap_matrix(True)
     for g in range(2):
         x = jnp.concatenate(
@@ -339,9 +343,8 @@
             ch = slice(32 * g + 16 * h, 32 * g + 16 * (h + 1))
             for a in range(16):
                 sg_out[ch, N2 * a : N2 * (a + 1)] = y[16 * a : 16 * (a + 1), h * N2 : (h + 1) * N2]
-    whole = (t_in[0] + t_in[1]) + (t_in[2] + t_in[3])
-    long_out[...] = whole[:4]
-    short_out[...] = whole[4:5]
+    long_out[...] = long_in[...]
+    short_out[...] = short_in[...]
 
 
 def shards(signal, grad_out, long_filter, short_filter, long_skip, short_skip):
@@ -351,22 +354,25 @@
     vmem = pl.BlockSpec(memory_space=pltpu.VMEM)
     V, S = pltpu.VMEM, pltpu.SMEM
     spec = V((N1, 2 * N2), F32)
-    raw_sg, raw_t = pl.pallas_call(
+    raw = pl.pallas_call(
         lambda *refs: kernel(n_ctx, n_tp, *refs),
         out_shape=(
             jax.ShapeDtypeStruct((64, 16, N2), BF16),
-            jax.ShapeDtypeStruct((4, 8, N2), F32),
+            jax.ShapeDtypeStruct((4, N2), F32),
+            jax.ShapeDtypeStruct((1, N2), F32),
         ),
         in_specs=[hbm] * 10,
-        out_specs=(vmem, vmem),
+        out_specs=(vmem, vmem, vmem),
         scratch_shapes=[
             V((64, 2048), BF16), V((64, 2048), BF16), V((16, N2), F32), V((2, 8, N2), F32),
             V((1, N2), F32), S((64,), F32), S((64,), F32),
             V((2 * N1, N1), BF16), V((N1, 2 * N1), BF16), V((N1, 2 * N2), F32), V((1536, 256), BF16),
             V((64, 2, 16, N2), BF16), V((2, 2, N1, N2), BF16), V((2, HALF + 8, N2), F32),
-            spec, spec, spec, spec, spec, spec, V((HALF + 8, N2), F32),
-            V((32, 24, N2), F32), V((32, 24, N2), F32), V((4, 8, N2), F32), V((2, 32, 16, N2), BF16),
-            pltpu.SemaphoreType.DMA((10,)), pltpu.SemaphoreType.DMA((6,)), pltpu.SemaphoreType.DMA((6,)),
+            spec, spec, spec, spec, V((HALF + 8, N2), F32),
+            V((768, N2), BF16), V((768, N2), BF16), V((N2, N1), F32),
+            V((N1, N2), F32), V((N1, N2), F32), V((1, N2), F32), V((128, N2), F32), V((2, 32, 16, N2), BF16),
+            pltpu.SemaphoreType.DMA((10,)), pltpu.SemaphoreType.DMA((7,)), pltpu.SemaphoreType.DMA((7,)),
+            pltpu.SemaphoreType.REGULAR,
         ],
         compiler_params=pltpu.CompilerParams(
             collective_id=0, has_side_effects=True, vmem_limit_bytes=60 * 1024 * 1024
@@ -383,9 +389,9 @@
             jax.ShapeDtypeStruct((4, N2), F32),
             jax.ShapeDtypeStruct((1, N2), F32),
         ),
-        in_specs=[vmem, vmem],
+        in_specs=[vmem, vmem, vmem],
         out_specs=(vmem, vmem, vmem),
-    )(raw_sg, raw_t)
+    )(*raw)
     return sg, long.reshape(512), short.reshape(N2)
 
 

time: 38 us -> 35.3 us (0.929)
  Pallas kernels: 37.3 us -> 34.5 us
    pallas_call x1, Pallas kernels: 35.4 us -> 32.6 us  [shards(): pl.pallas_call(lambda *refs: kernel(n_ctx, n_tp, *refs), out_shape=(jax.S...]
where the time goes in v3:
time: 35.3 us; the launch traced here: 35.1 us
  Pallas kernels  34.5 us (98%)
  between operations  0.64 us (2%)
    pallas_call x1, Pallas kernels, shards(): pl.pallas_call(lambda *refs: kernel(n_ctx, n_tp, *refs), out_shape=(jax.S...  32.6 us
    pallas_call x1, Pallas kernels, shards(): pl.pallas_call(lay_out, out_shape=(jax.ShapeDtypeStruct((64, 2048), BF16)...  1.9 us

profile of v3, /device:TPU:1, one launch (start us, length us, event | category | flops | bytes accessed | tf_op | source)
XLA Modules:
  0.0 35.1 jit_solution(1761636378302648717)
XLA Ops:
  0.6 32.6 %shard_map.121 = (bf16[64,16,128]{2,1,0:T(8,128)(2,1)}, f32[4,128]{1,0:T(4,128)}, f32[1,128]{1,0:T(1,128)}) custom-call(bf16[64,2048]{1,0:T(8,128)(2,1)} %refs_0_.1, bf16[64,2048]{1,0:T(8,128)(2,1)} %refs_1_.1, f32[16,128]{1,0:T(8,128)} %bitcast.4, f32[1,128]{1,0:T(1,128)} %bitcast.6, f32[64]{0:T(128)} %refs_4_.1, f32[64]{0:T(128)} %refs_5_.1, ...), custom_call_target="tpu_custom_call" | custom-call | flops 6000000000 | bytes 8000000 | tf_op jit(solution)/shard_map/pallas_call | solution.py:357
  33.2 1.9 %shard_map.122 = (bf16[64,2048]{1,0:T(8,128)(2,1)}, f32[4,128]{1,0:T(4,128)}, f32[1,128]{1,0:T(1,128)}) custom-call(bf16[64,16,128]{2,1,0:T(8,128)(2,1)} %get-tuple-element.9.sg_in, f32[4,128]{1,0:T(4,128)} %get-tuple-element.10.long_in, f32[1,128]{1,0:T(1,128)} %get-tuple-element.11.short_in), custom_call_target="tpu_custom_call" | custom-call | tf_op jit(solution)/shard_map/pallas_call | solution.py:385

commit v4 on v3

v4 whole, which is shorter than its diff:
```python
import math

import jax
import jax.numpy as jnp
import ml_dtypes
import numpy as np
from jax import lax
from jax.experimental import pallas as pl
from jax.experimental.pallas import tpu as pltpu
from jax.sharding import PartitionSpec as P

MESH = pl.DeviceIdType.MESH
F32, BF16 = jnp.float32, jnp.bfloat16
N1, N2 = 512, 128
LEN = N1 * N2
HALF = N1 // 2


def split_np(x):
    x = x.astype(np.float32)
    hi = x.astype(ml_dtypes.bfloat16)
    lo = (x - hi.astype(np.float32)).astype(ml_dtypes.bfloat16)
    return hi, lo


def tables():
    k = np.arange(N1, dtype=np.float64)[:, None] + 0.25
    kh = k[:HALF]
    fwd, inv = [], []
    for odd in range(2):
        n = 2 * np.arange(HALF, dtype=np.float64)[None, :] + odd
        ang = -2 * np.pi * np.mod(kh * n, N1) / N1
        hi, lo = split_np(np.concatenate([np.cos(ang), np.sin(ang)], axis=0))
        fwd.append(np.concatenate([hi, lo], axis=1))
        inv.append(np.concatenate([hi.T, lo.T], axis=1))
    m = np.arange(N2, dtype=np.float64)
    ang = -2 * np.pi * k * m[None, :] / LEN
    twist = np.concatenate([np.cos(ang), np.sin(ang)], axis=1)
    ang = np.broadcast_to(-2 * np.pi * kh / N1, (HALF, N2))
    twist = np.concatenate([twist, np.concatenate([np.cos(ang), np.sin(ang)], axis=1)]).astype(np.float32)
    ang = -2 * np.pi * np.mod(m[:, None] * m[None, :], N2) / N2
    br, bi = np.cos(ang), np.sin(ang)
    b_hi, b_lo = split_np(np.block([[br, bi], [-bi, br]]))
    c_hi, c_lo = split_np(np.block([[br, -bi], [bi, br]]) / LEN)
    mix = np.concatenate([b_hi, b_hi, b_lo, c_hi, c_hi, c_lo])
    return np.concatenate(fwd), np.concatenate(inv), twist, mix


def dot(a, b):
    return jnp.dot(a, b, preferred_element_type=F32)


def split(x):
    hi = x.astype(BF16)
    return hi, (x - hi.astype(F32)).astype(BF16)


def split3(x):
    hi, lo = split(x)
    return jnp.concatenate([hi, lo, hi], axis=1)


def twice(x):
    return jnp.concatenate([x, x], axis=0)


def mix_forward(even, odd, twist, mix, z_refs):
    for q, z in enumerate(z_refs):
        s = slice(q * N2, (q + 1) * N2)
        er, ei, dr, di = even[:HALF, s], even[HALF:, s], odd[:HALF, s], odd[HALF:, s]
        for h, (xr, xi) in enumerate([(er + dr, ei + di), (er - dr, ei - di)]):
            r = slice(h * HALF, (h + 1) * HALF)
            tr, ti = twist[r, :N2], twist[r, N2:]
            y = jnp.concatenate([xr * tr - xi * ti, xi * tr + xr * ti], axis=1)
            z[r, :] = dot(split3(y), mix[:768, :])


def forward_exact(xe, xo, fwd, twist, mix, z_refs):
    mix_forward(dot(fwd[:N1, :], twice(xe)), dot(fwd[N1:, :], twice(xo)), twist, mix, z_refs)


def forward_filter(fe, fo, fwd, twist, mix, z):
    hi, lo = split(jnp.concatenate([fe, fo], axis=1))
    y = dot(fwd[:N1, :], twice(hi)) + dot(fwd[:N1, :HALF], lo)
    tr, ti = twist[N1:, :N2], twist[N1:, N2:]
    dr, di = y[:HALF, N2:], y[HALF:, N2:]
    odd = jnp.concatenate([dr * tr - di * ti, di * tr + dr * ti], axis=0)
    mix_forward(y[:, :N2], odd, twist, mix, (z,))


def inverse_pair(left, right, inv, twist, mix):
    plus, minus = [], []
    for a, b in zip(left, right):
        ys = []
        for h in range(2):
            r = slice(h * HALF, (h + 1) * HALF)
            ar, ai = a[r, :N2], a[r, N2:]
            br, bi = b(r)
            z = jnp.concatenate([ar * br + ai * bi, ai * br - ar * bi], axis=1)
            y = dot(split3(z), mix[768:, :])
            yr, yi = y[:, :N2], y[:, N2:]
            tr, ti = twist[r, :N2], twist[r, N2:]
            ys.append(jnp.concatenate([yr * tr + yi * ti, yi * tr - yr * ti], axis=0))
        plus.append(ys[0] + ys[1])
        minus.append(ys[0] - ys[1])
    out = []
    for h, y in enumerate((plus, minus)):
        hi, lo = split(jnp.concatenate(y, axis=1))
        r = slice(h * HALF, (h + 1) * HALF)
        out.append(dot(inv[r, :], twice(hi)) + dot(inv[r, :N1], lo))
    return out


def one_hot(cond):
    return jnp.where(cond, 1.0, 0.0).astype(BF16)


def swap_matrix(back):
    i = lax.broadcasted_iota(jnp.int32, (256, 256), 0)
    j = lax.broadcasted_iota(jnp.int32, (256, 256), 1)
    if back:
        i, j = j, i
    p = i % 16
    return one_hot((i // 16 == j % 16) & (2 * (p % 8) + p // 8 == j // 16))


def rolled(w_row, first, rows):
    zero = jnp.zeros((1, N2), F32)
    base = jnp.concatenate([w_row, zero] if first else [zero, w_row], axis=1)
    return pltpu.roll(jnp.broadcast_to(base, (rows, 2 * N2)), 0, 1, stride=1, stride_axis=0)


def stack3(x):
    hi, lo = split(x)
    return jnp.concatenate([hi, hi, lo], axis=0)


def long_rows(re, ro, r_buf, band, alpha):
    se, so = re[0] + re[1], ro[0] + ro[1]
    r_buf[:HALF, :] = se
    pair = jnp.concatenate(
        [jnp.concatenate([se, so], axis=1), jnp.concatenate([so, r_buf[pl.ds(1, HALF), :]], axis=1)], axis=0
    )
    long = dot(split3(pair), band)
    long_e = long[:HALF] + (alpha[0] * re[0] + alpha[1] * re[1])
    long_o = long[HALF:] + (alpha[0] * ro[0] + alpha[1] * ro[1])
    return long_e, long_o, pair


def turned_filter(fe, fo):
    i = lax.broadcasted_iota(jnp.int32, (N2, N2), 0)
    j = lax.broadcasted_iota(jnp.int32, (N2, N2), 1)
    flip = one_hot(i + j == N2 - 1)
    hi, lo = split(jnp.transpose(jnp.concatenate([fe, fo], axis=0)))
    return dot(flip, hi).astype(BF16), dot(flip, lo).astype(BF16)


def short_row(pair, f_hi, f_lo, re, lam):
    hi, lo = split(pair)
    cross = dot(f_hi, hi) + (dot(f_hi, lo) + dot(f_lo, hi))
    diag = pltpu.roll(cross, N2 + 1, 1, stride=1, stride_axis=0)
    short = jnp.sum(diag, axis=0, keepdims=True)[:, :N2]
    return short + (lam[0] * re[0][:1, :] + lam[1] * re[1][:1, :])


def whole(z):
    return lambda r: (z[r, :N2], z[r, N2:])


def filter_product(zf, zw, lam, alpha):
    def rows(r):
        fr, fi = zf[r, :N2] + lam, zf[r, N2:]
        wr, wi = zw[r, :N2] + alpha, zw[r, N2:]
        return fr * wr - fi * wi, fr * wi + fi * wr

    return rows


def tail_matrix(f_last, band):
    tail = dot(split3(f_last), band)
    i = lax.broadcasted_iota(jnp.int32, (N2, N2), 0)
    j = lax.broadcasted_iota(jnp.int32, (N2, N2), 1)
    flip = one_hot(i + j == N2)
    hi, lo = split(tail)
    turned = (dot(hi, flip) + dot(lo, flip))[7:, :]
    return rolled(turned, True, N2)[:, :N2]


def halves(x):
    x = x.astype(F32).reshape(32, 16, N2)
    return x[:, :8].reshape(HALF, N2).astype(BF16), x[:, 8:].reshape(HALF, N2).astype(BF16)


def offsets():
    def far(o):
        return o[0] + min(o[1], 4 - o[1]) + min(o[2], 4 - o[2])

    out = [(y, z, x) for y in range(2) for z in range(4) for x in range(4)][1:]
    return sorted(out, key=lambda o: -far(o))


def all_offsets():
    def far(o):
        y = (1 if o[1] else 2) if o[0] & 2 else o[1]
        return y + min(o[2], 4 - o[2]) + min(o[3], 4 - o[3])

    out = [(t, y, z, x) for y in range(2) for z in range(4) for x in range(4) for t in range(4)][1:]
    return sorted(out, key=lambda o: -far(o))


def kernel(
    n_ctx, n_tp,
    sig, cot, filt, w_in, lam_in, alpha_in, f_tab, i_tab, t_tab, m_tab,
    sg_recv, long_out, short_out,
    sig_v, cot_v, filt_v, filt_s, w_v, lam_s, alpha_s, fwd, inv, twist, mix,
    send, recv, f_buf, zs0, zg0, zs1, zg1, zf, r_buf, band_a, band_c, zw,
    l_rows, l_send, l_recv, s_send, s_recv, sg_send, load_sem, send_sem, recv_sem, ready,
):
    me, tp = lax.axis_index("ctx"), lax.axis_index("tp")
    zs, zg = (zs0, zs1), (zg0, zg1)
    my_y, my_z, my_x = me // 16, (me // 4) % 4, me % 4
    at = {(y, z, x): (my_y ^ y) * 16 + ((my_z + z) & 3) * 4 + ((my_x + x) & 3) for y, z, x in [(0, 0, 0)] + offsets()}
    peers = [at[o] for o in offsets()]
    tp_peers = [tp ^ i for i in (3, 2, 1)]
    n_peers = len(peers)
    n_all = n_ctx * n_tp
    my_id = n_tp * me + tp

    barrier = pltpu.get_barrier_semaphore()
    for e in peers:
        pl.semaphore_signal(barrier, inc=1, device_id={"ctx": e}, device_id_type=MESH)
    for t in tp_peers:
        pl.semaphore_signal(barrier, inc=1, device_id={"tp": t}, device_id_type=MESH)
    loads = [
        pltpu.make_async_copy(src, dst, load_sem.at[i])
        for i, (src, dst) in enumerate(
            [(filt, filt_v), (sig, sig_v), (cot, cot_v), (w_in, w_v), (lam_in, lam_s), (alpha_in, alpha_s),
             (f_tab, fwd), (t_tab, twist), (m_tab, mix), (i_tab, inv)]
        )
    ]
    for c in loads:
        c.start()
    r_buf[HALF:, :] = jnp.zeros((8, N2), F32)
    swap = swap_matrix(False)
    for c in loads[:6]:
        c.wait()
    for h in range(2):
        for i in range(8):
            filt_s[h, i : i + 1, :] = filt_v[2 * i + h : 2 * i + h + 1, :]
    for g in range(4):
        ch = slice(16 * g, 16 * (g + 1))
        x = jnp.concatenate(
            [
                jnp.concatenate([v[ch, N2 * a : N2 * (a + 1)] for a in range(16)], axis=0)
                for v in (sig_v, cot_v)
            ],
            axis=1,
        )
        y = dot(swap, x).astype(BF16)
        send[ch, 0] = y[:, :N2].reshape(16, 16, N2)
        send[ch, 1] = y[:, N2:].reshape(16, 16, N2)
    pl.semaphore_wait(barrier, n_peers + len(tp_peers))
    for t in tp_peers:
        pl.semaphore_signal(ready, inc=1, device_id={"tp": t}, device_id_type=MESH)

    rows_me = pl.ds(pl.multiple_of(16 * me, 16), 16)
    f_dst = f_buf.at[:, pl.ds(pl.multiple_of(8 * me, 8), 8), :]

    def remote(src, dst, k, where):
        pltpu.make_async_remote_copy(
            src_ref=src, dst_ref=dst, send_sem=send_sem.at[k], recv_sem=recv_sem.at[k],
            device_id=where, device_id_type=MESH,
        ).start()

    def local(src, dst, k):
        pltpu.make_async_copy(src, dst, recv_sem.at[k]).start()

    def finish(ref, sem):
        pltpu.make_async_copy(ref, ref, sem).wait()

    for c in range(2):
        for e in peers:
            remote(send.at[2 * e + c], recv.at[c, :, rows_me, :], 1 + c, {"ctx": e})
    for e in peers:
        remote(filt_s, f_dst, 0, {"ctx": e})
    for c in range(2):
        local(send.at[2 * me + c], recv.at[c, :, rows_me, :], 1 + c)
    local(filt_s, f_dst, 0)

    w_row = w_v[...]
    band_a[...] = stack3(jnp.transpose(rolled(w_row, True, N2)))
    band_c[...] = stack3(rolled(w_row, False, N2)[:, :N2])
    alpha = (alpha_s[2 * me], alpha_s[2 * me + 1])
    lam = (lam_s[2 * me], lam_s[2 * me + 1])
    for c in loads[6:]:
        c.wait()
    zw[...] = dot(split3(twist[:N1, :] * jnp.concatenate([w_row, w_row], axis=1)), mix[:768, :])

    for c in range(2):
        finish(recv.at[c], recv_sem.at[1 + c])
        se, so = halves(recv[c, 0])
        ge, go = halves(recv[c, 1])
        forward_exact(
            jnp.concatenate([se, ge], axis=1), jnp.concatenate([so, go], axis=1), fwd, twist, mix, (zs[c], zg[c])
        )
    even, odd = inverse_pair(zg, [whole(z) for z in zs], inv, twist, mix)
    re, ro = (even[:, :N2], even[:, N2:]), (odd[:, :N2], odd[:, N2:])
    long_e, long_o, pair = long_rows(re, ro, r_buf, band_a[...], alpha)
    l_rows[pl.ds(0, HALF, 2), :] = long_e
    l_rows[pl.ds(1, HALF, 2), :] = long_o
    l_send[...] = l_rows[...].reshape(128, 4, N2)
    pl.semaphore_wait(ready, len(tp_peers))
    everyone = [(at[o[1:]], tp ^ o[0]) for o in all_offsets()]
    for e, t in everyone:
        remote(l_send.at[n_tp * e + t], l_recv.at[my_id], 5, {"ctx": e, "tp": t})
    local(l_send.at[my_id], l_recv.at[my_id], 5)

    finish(f_buf, recv_sem.at[0])
    fe, fo = f_buf[0], f_buf[1]
    ft_hi, ft_lo = turned_filter(fe, fo)
    s_send[...] = short_row(pair, ft_hi, ft_lo, re, lam)
    for e, t in everyone:
        remote(s_send, s_recv.at[my_id], 6, {"ctx": e, "tp": t})
    local(s_send, s_recv.at[my_id], 6)
    forward_filter(fe, fo, fwd, twist, mix, zf)
    t_hi, t_lo = split(tail_matrix(fo[HALF - 8 :, :], band_c[...]))
    even, odd = inverse_pair(
        zg, [filter_product(zf, zw, lam[c], alpha[c]) for c in range(2)], inv, twist, mix
    )
    for c in range(2):
        s = slice(c * N2, (c + 1) * N2)
        first = recv[c, 1, :16, :]
        fold = (dot(first, t_hi) + dot(first, t_lo))[:1, :]
        last = jnp.concatenate([odd[: HALF - 1, s], odd[HALF - 1 :, s] + fold], axis=0)
        rows = [x.reshape(32, 8, N2) for x in (even[:, s], last)]
        sg_send[c] = jnp.concatenate(rows, axis=1).astype(BF16)
    sg_dst = sg_recv.at[pl.ds(2 * me, 2)]
    for e in peers:
        remote(sg_send.at[:, e], sg_dst, 3, {"ctx": e})
    local(sg_send.at[:, me], sg_dst, 3)

    finish(l_recv, recv_sem.at[5])
    long_out[...] = jnp.sum(l_recv[...], axis=0)
    finish(s_recv, recv_sem.at[6])
    short_out[...] = jnp.sum(s_recv[...], axis=0)
    finish(sg_recv, recv_sem.at[3])
    finish(f_buf.at[:, pl.ds(0, 8 * n_peers), :], send_sem.at[0])
    for c in range(2):
        finish(send.at[pl.ds(0, n_peers)], send_sem.at[1 + c])
    finish(sg_send.at[:, pl.ds(0, n_peers)], send_sem.at[3])
    finish(l_send.at[pl.ds(0, n_all - 1)], send_sem.at[5])
    finish(s_recv.at[pl.ds(0, n_all - 1)], send_sem.at[6])


def lay_out(sg_in, long_in, short_in, sg_out, long_out, short_out, rows, sem):
    swap = swap_matrix(True)
    copies = [
        pltpu.make_async_copy(long_in, long_out, sem.at[2]),
        pltpu.make_async_copy(short_in, short_out, sem.at[3]),
    ]
    for c in copies:
        c.start()
    for g in range(2):
        x = jnp.concatenate(
            [sg_in[32 * g + 16 * h : 32 * g + 16 * (h + 1)].reshape(256, N2) for h in range(2)], axis=1
        )
        y = dot(swap, x).astype(BF16)
        for h in range(2):
            ch = slice(32 * g + 16 * h, 32 * g + 16 * (h + 1))
            for a in range(16):
                rows[ch, N2 * a : N2 * (a + 1)] = y[16 * a : 16 * (a + 1), h * N2 : (h + 1) * N2]
        part = pl.ds(32 * g, 32)
        copies.append(pltpu.make_async_copy(rows.at[part, :], sg_out.at[part, :], sem.at[g]))
        copies[-1].start()
    for c in copies:
        c.wait()


def shards(signal, grad_out, long_filter, short_filter, long_skip, short_skip):
    n_ctx, n_tp = lax.axis_size("ctx"), lax.axis_size("tp")
    consts = [jnp.asarray(t) for t in tables()]
    hbm = pl.BlockSpec(memory_space=pltpu.HBM)
    vmem = pl.BlockSpec(memory_space=pltpu.VMEM)
    V, S = pltpu.VMEM, pltpu.SMEM
    spec = V((N1, 2 * N2), F32)
    raw = pl.pallas_call(
        lambda *refs: kernel(n_ctx, n_tp, *refs),
        out_shape=(
            pltpu.VMEM((64, 16, N2), BF16),
            pltpu.VMEM((4, N2), F32),
            pltpu.VMEM((1, N2), F32),
        ),
        in_specs=[hbm] * 10,
        out_specs=(vmem, vmem, vmem),
        scratch_shapes=[
            V((64, 2048), BF16), V((64, 2048), BF16), V((16, N2), F32), V((2, 8, N2), F32),
            V((1, N2), F32), S((64,), F32), S((64,), F32),
            V((2 * N1, N1), BF16), V((N1, 2 * N1), BF16), V((768, 2 * N2), F32), V((1536, 256), BF16),
            V((64, 2, 16, N2), BF16), V((2, 2, N1, N2), BF16), V((2, HALF, N2), F32),
            spec, spec, spec, spec, spec, V((HALF + 8, N2), F32),
            V((768, N2), BF16), V((384, N2), BF16), spec,
            V((N1, N2), F32), V((128, 4, N2), F32), V((128, 4, N2), F32), V((1, N2), F32), V((128, 1, N2), F32), V((2, 32, 16, N2), BF16),
            pltpu.SemaphoreType.DMA((10,)), pltpu.SemaphoreType.DMA((7,)), pltpu.SemaphoreType.DMA((7,)),
            pltpu.SemaphoreType.REGULAR,
        ],
        compiler_params=pltpu.CompilerParams(
            collective_id=0, has_side_effects=True, vmem_limit_bytes=60 * 1024 * 1024
        ),
        cost_estimate=pl.CostEstimate(flops=6_000_000_000, bytes_accessed=8_000_000, transcendentals=0),
    )(
        signal, grad_out, long_filter.reshape(16, N2), short_filter.reshape(1, N2),
        long_skip, short_skip, *consts,
    )
    sg, long, short = pl.pallas_call(
        lay_out,
        out_shape=(
            jax.ShapeDtypeStruct((64, 2048), BF16),
            jax.ShapeDtypeStruct((4, N2), F32),
            jax.ShapeDtypeStruct((1, N2), F32),
        ),
        in_specs=[vmem, vmem, vmem],
        out_specs=(hbm, hbm, hbm),
        scratch_shapes=[V((64, 2048), BF16), pltpu.SemaphoreType.DMA((4,))],
    )(*[pltpu.with_memory_space_constraint(r, pltpu.VMEM) for r in raw])
    return sg, long.reshape(512), short.reshape(N2)


def solution(mesh):
    placed = (P("tp", "ctx"), P("tp", "ctx"), P("ctx"), P(), P("tp"), P("tp"))
    return jax.shard_map(
        shards,
        mesh=mesh,
        in_specs=placed,
        out_specs=(P("tp", "ctx"), P(("ctx", "tp")), P()),
        check_vma=False,
    )
```

time: 35.3 us -> 31.4 us (0.89)
  the two profiles are of different devices: /device:TPU:1 before, /device:TPU:0 now
where the time goes in v4:
time: 31.4 us; the launch traced here: 31.3 us
  Pallas kernels  30.6 us (97%)
  between operations  0.64 us (2%)
    pallas_call x1, Pallas kernels, shards(): pl.pallas_call(lambda *refs: kernel(n_ctx, n_tp, *refs), out_shape=(pltpu...  29.6 us
    pallas_call x1, Pallas kernels, shards(): pl.pallas_call(lay_out, out_shape=(jax.ShapeDtypeStruct((64, 2048), BF16)...  0.97 us

profile of v4, /device:TPU:0, one launch (start us, length us, event | category | flops | bytes accessed | tf_op | source)
XLA Modules:
  0.0 31.3 jit_solution(11716960645118486121)
XLA Ops:
  0.6 29.6 %shard_map.121 = (bf16[64,16,128]{2,1,0:T(8,128)(2,1)S(1)}, f32[4,128]{1,0:T(4,128)S(1)}, f32[1,128]{1,0:T(1,128)S(1)}) custom-call(bf16[64,2048]{1,0:T(8,128)(2,1)} %refs_0_.1, bf16[64,2048]{1,0:T(8,128)(2,1)} %refs_1_.1, f32[16,128]{1,0:T(8,128)} %bitcast.4, f32[1,128]{1,0:T(1,128)} %bitcast.6, f32[64]{0:T(128)} %refs_4_.1, f32[64]{0:T(128)} %refs_5_.1, ...), custom_call_target="tpu_custom_call" | custom-call | flops 6000000000 | bytes 8000000 | tf_op jit(solution)/shard_map/pallas_call | solution.py:386
  30.3 1.0 %shard_map.122 = (bf16[64,2048]{1,0:T(8,128)(2,1)}, f32[4,128]{1,0:T(4,128)}, f32[1,128]{1,0:T(1,128)}) custom-call(bf16[64,16,128]{2,1,0:T(8,128)(2,1)S(1)} %get-tuple-element.9.sg_in, f32[4,128]{1,0:T(4,128)S(1)} %get-tuple-element.10.long_in, f32[1,128]{1,0:T(1,128)S(1)} %get-tuple-element.11.short_in), custom_call_target="tpu_custom_call" | custom-call | tf_op jit(solution)/shard_map/pallas_call | solution.py:414

commit v5 on v4

--- a/solution.py
+++ b/solution.py
@@ -81,31 +81,31 @@
 
 def forward_filter(fe, fo, fwd, twist, mix, z):
     hi, lo = split(jnp.concatenate([fe, fo], axis=1))
-    y = dot(fwd[:N1, :], twice(hi)) + dot(fwd[:N1, :HALF], lo)
+    yr, yi = (dot(fwd[r, :], twice(hi)) + dot(fwd[r, :HALF], lo) for r in (slice(0, HALF), slice(HALF, N1)))
     tr, ti = twist[N1:, :N2], twist[N1:, N2:]
-    dr, di = y[:HALF, N2:], y[HALF:, N2:]
+    dr, di = yr[:, N2:], yi[:, N2:]
+    even = jnp.concatenate([yr[:, :N2], yi[:, :N2]], axis=0)
     odd = jnp.concatenate([dr * tr - di * ti, di * tr + dr * ti], axis=0)
-    mix_forward(y[:, :N2], odd, twist, mix, (z,))
-
-
-def inverse_pair(left, right, inv, twist, mix):
-    plus, minus = [], []
-    for a, b in zip(left, right):
-        ys = []
-        for h in range(2):
-            r = slice(h * HALF, (h + 1) * HALF)
-            ar, ai = a[r, :N2], a[r, N2:]
-            br, bi = b(r)
-            z = jnp.concatenate([ar * br + ai * bi, ai * br - ar * bi], axis=1)
-            y = dot(split3(z), mix[768:, :])
-            yr, yi = y[:, :N2], y[:, N2:]
-            tr, ti = twist[r, :N2], twist[r, N2:]
-            ys.append(jnp.concatenate([yr * tr + yi * ti, yi * tr - yr * ti], axis=0))
-        plus.append(ys[0] + ys[1])
-        minus.append(ys[0] - ys[1])
+    mix_forward(even, odd, twist, mix, (z,))
+
+
+def inverse_mix(a, b, twist, mix):
+    ys = []
+    for h in range(2):
+        r = slice(h * HALF, (h + 1) * HALF)
+        ar, ai, br, bi = a[r, :N2], a[r, N2:], b[r, :N2], b[r, N2:]
+        z = jnp.concatenate([ar * br + ai * bi, ai * br - ar * bi], axis=1)
+        y = dot(split3(z), mix[768:, :])
+        yr, yi = y[:, :N2], y[:, N2:]
+        tr, ti = twist[r, :N2], twist[r, N2:]
+        ys.append(jnp.concatenate([yr * tr + yi * ti, yi * tr - yr * ti], axis=0))
+    return ys[0] + ys[1], ys[0] - ys[1]
+
+
+def inverse_rows(halves, inv):
     out = []
-    for h, y in enumerate((plus, minus)):
-        hi, lo = split(jnp.concatenate(y, axis=1))
+    for h in range(2):
+        hi, lo = split(jnp.concatenate([x[h] for x in halves], axis=1))
         r = slice(h * HALF, (h + 1) * HALF)
         out.append(dot(inv[r, :], twice(hi)) + dot(inv[r, :N1], lo))
     return out
@@ -163,17 +163,11 @@
     return short + (lam[0] * re[0][:1, :] + lam[1] * re[1][:1, :])
 
 
-def whole(z):
-    return lambda r: (z[r, :N2], z[r, N2:])
-
-
-def filter_product(zf, zw, lam, alpha):
-    def rows(r):
-        fr, fi = zf[r, :N2] + lam, zf[r, N2:]
-        wr, wi = zw[r, :N2] + alpha, zw[r, N2:]
-        return fr * wr - fi * wi, fr * wi + fi * wr
-
-    return rows
+def filter_product(zf, zw, lam, alpha, zv):
+    fr, fi = zf[:, :N2] + lam, zf[:, N2:]
+    wr, wi = zw[:, :N2] + alpha, zw[:, N2:]
+    zv[:, :N2] = fr * wr - fi * wi
+    zv[:, N2:] = fr * wi + fi * wr
 
 
 def tail_matrix(f_last, band):
@@ -213,11 +207,11 @@
     sig, cot, filt, w_in, lam_in, alpha_in, f_tab, i_tab, t_tab, m_tab,
     sg_recv, long_out, short_out,
     sig_v, cot_v, filt_v, filt_s, w_v, lam_s, alpha_s, fwd, inv, twist, mix,
-    send, recv, f_buf, zs0, zg0, zs1, zg1, zf, r_buf, band_a, band_c, zw,
+    send, recv, f_buf, zs0, zg0, zs1, zg1, zf, zv0, zv1, half, r_buf, band_a, band_c, zw,
     l_rows, l_send, l_recv, s_send, s_recv, sg_send, load_sem, send_sem, recv_sem, ready,
 ):
     me, tp = lax.axis_index("ctx"), lax.axis_index("tp")
-    zs, zg = (zs0, zs1), (zg0, zg1)
+    zs, zg, zv = (zs0, zs1), (zg0, zg1), (zv0, zv1)
     my_y, my_z, my_x = me // 16, (me // 4) % 4, me % 4
     at = {(y, z, x): (my_y ^ y) * 16 + ((my_z + z) & 3) * 4 + ((my_x + x) & 3) for y, z, x in [(0, 0, 0)] + offsets()}
     peers = [at[o] for o in offsets()]
@@ -303,7 +297,10 @@
         forward_exact(
             jnp.concatenate([se, ge], axis=1), jnp.concatenate([so, go], axis=1), fwd, twist, mix, (zs[c], zg[c])
         )
-    even, odd = inverse_pair(zg, [whole(z) for z in zs], inv, twist, mix)
+        part = inverse_mix(zg[c], zs[c], twist, mix)
+        if c == 0:
+            half[0], half[1] = part
+    even, odd = inverse_rows([(half[0], half[1]), part], inv)
     re, ro = (even[:, :N2], even[:, N2:]), (odd[:, :N2], odd[:, N2:])
     long_e, long_o, pair = long_rows(re, ro, r_buf, band_a[...], alpha)
     l_rows[pl.ds(0, HALF, 2), :] = long_e
@@ -324,9 +321,9 @@
     local(s_send, s_recv.at[my_id], 6)
     forward_filter(fe, fo, fwd, twist, mix, zf)
     t_hi, t_lo = split(tail_matrix(fo[HALF - 8 :, :], band_c[...]))
-    even, odd = inverse_pair(
-        zg, [filter_product(zf, zw, lam[c], alpha[c]) for c in range(2)], inv, twist, mix
-    )
+    for c in range(2):
+        filter_product(zf, zw, lam[c], alpha[c], zv[c])
+    even, odd = inverse_rows([inverse_mix(zg[c], zv[c], twist, mix) for c in range(2)], inv)
     for c in range(2):
         s = slice(c * N2, (c + 1) * N2)
         first = recv[c, 1, :16, :]
@@ -397,7 +394,7 @@
             V((1, N2), F32), S((64,), F32), S((64,), F32),
             V((2 * N1, N1), BF16), V((N1, 2 * N1), BF16), V((768, 2 * N2), F32), V((1536, 256), BF16),
             V((64, 2, 16, N2), BF16), V((2, 2, N1, N2), BF16), V((2, HALF, N2), F32),
-            spec, spec, spec, spec, spec, V((HALF + 8, N2), F32),
+            spec, spec, spec, spec, spec, spec, spec, V((2, N1, N2), F32), V((HALF + 8, N2), F32),
             V((768, N2), BF16), V((384, N2), BF16), spec,
             V((N1, N2), F32), V((128, 4, N2), F32), V((128, 4, N2), F32), V((1, N2), F32), V((128, 1, N2), F32), V((2, 32, 16, N2), BF16),
             pltpu.SemaphoreType.DMA((10,)), pltpu.SemaphoreType.DMA((7,)), pltpu.SemaphoreType.DMA((7,)),

time: 31.4 us -> 31.1 us (level)
  no operation moved by 1% of the time
where the time goes in v5:
time: 31.1 us; the launch traced here: 31 us
  Pallas kernels  30.3 us (97%)
  between operations  0.64 us (2%)
    pallas_call x1, Pallas kernels, shards(): pl.pallas_call(lambda *refs: kernel(n_ctx, n_tp, *refs), out_shape=(pltpu...  29.3 us
    pallas_call x1, Pallas kernels, shards(): pl.pallas_call(lay_out, out_shape=(jax.ShapeDtypeStruct((64, 2048), BF16)...  0.97 us

profile of v5, /device:TPU:0, one launch (start us, length us, event | category | flops | bytes accessed | tf_op | source)
XLA Modules:
  0.0 31.0 jit_solution(1485143924689087425)
XLA Ops:
  0.6 29.3 %shard_map.121 = (bf16[64,16,128]{2,1,0:T(8,128)(2,1)S(1)}, f32[4,128]{1,0:T(4,128)S(1)}, f32[1,128]{1,0:T(1,128)S(1)}) custom-call(bf16[64,2048]{1,0:T(8,128)(2,1)} %refs_0_.1, bf16[64,2048]{1,0:T(8,128)(2,1)} %refs_1_.1, f32[16,128]{1,0:T(8,128)} %bitcast.4, f32[1,128]{1,0:T(1,128)} %bitcast.6, f32[64]{0:T(128)} %refs_4_.1, f32[64]{0:T(128)} %refs_5_.1, ...), custom_call_target="tpu_custom_call" | custom-call | flops 6000000000 | bytes 8000000 | tf_op jit(solution)/shard_map/pallas_call | solution.py:383
  30.0 1.0 %shard_map.122 = (bf16[64,2048]{1,0:T(8,128)(2,1)}, f32[4,128]{1,0:T(4,128)}, f32[1,128]{1,0:T(1,128)}) custom-call(bf16[64,16,128]{2,1,0:T(8,128)(2,1)S(1)} %get-tuple-element.9.sg_in, f32[4,128]{1,0:T(4,128)S(1)} %get-tuple-element.10.long_in, f32[1,128]{1,0:T(1,128)S(1)} %get-tuple-element.11.short_in), custom_call_target="tpu_custom_call" | custom-call | tf_op jit(solution)/shard_map/pallas_call | solution.py:411

commit v6 on v5

--- a/solution.py
+++ b/solution.py
@@ -181,7 +181,7 @@
 
 
 def halves(x):
-    x = x.astype(F32).reshape(32, 16, N2)
+    x = x.astype(F32)
     return x[:, :8].reshape(HALF, N2).astype(BF16), x[:, 8:].reshape(HALF, N2).astype(BF16)
 
 
@@ -208,7 +208,7 @@
     sg_recv, long_out, short_out,
     sig_v, cot_v, filt_v, filt_s, w_v, lam_s, alpha_s, fwd, inv, twist, mix,
     send, recv, f_buf, zs0, zg0, zs1, zg1, zf, zv0, zv1, half, r_buf, band_a, band_c, zw,
-    l_rows, l_send, l_recv, s_send, s_recv, sg_send, load_sem, send_sem, recv_sem, ready,
+    l_send, l_recv, s_send, s_recv, sg_send, load_sem, send_sem, recv_sem, ready,
 ):
     me, tp = lax.axis_index("ctx"), lax.axis_index("tp")
     zs, zg, zv = (zs0, zs1), (zg0, zg1), (zv0, zv1)
@@ -257,8 +257,7 @@
     for t in tp_peers:
         pl.semaphore_signal(ready, inc=1, device_id={"tp": t}, device_id_type=MESH)
 
-    rows_me = pl.ds(pl.multiple_of(16 * me, 16), 16)
-    f_dst = f_buf.at[:, pl.ds(pl.multiple_of(8 * me, 8), 8), :]
+    f_dst = f_buf.at[me]
 
     def remote(src, dst, k, where):
         pltpu.make_async_remote_copy(
@@ -274,11 +273,11 @@
 
     for c in range(2):
         for e in peers:
-            remote(send.at[2 * e + c], recv.at[c, :, rows_me, :], 1 + c, {"ctx": e})
+            remote(send.at[2 * e + c], recv.at[c, me], 1 + c, {"ctx": e})
     for e in peers:
         remote(filt_s, f_dst, 0, {"ctx": e})
     for c in range(2):
-        local(send.at[2 * me + c], recv.at[c, :, rows_me, :], 1 + c)
+        local(send.at[2 * me + c], recv.at[c, me], 1 + c)
     local(filt_s, f_dst, 0)
 
     w_row = w_v[...]
@@ -292,8 +291,8 @@
 
     for c in range(2):
         finish(recv.at[c], recv_sem.at[1 + c])
-        se, so = halves(recv[c, 0])
-        ge, go = halves(recv[c, 1])
+        se, so = halves(recv[c, :, 0])
+        ge, go = halves(recv[c, :, 1])
         forward_exact(
             jnp.concatenate([se, ge], axis=1), jnp.concatenate([so, go], axis=1), fwd, twist, mix, (zs[c], zg[c])
         )
@@ -303,17 +302,18 @@
     even, odd = inverse_rows([(half[0], half[1]), part], inv)
     re, ro = (even[:, :N2], even[:, N2:]), (odd[:, :N2], odd[:, N2:])
     long_e, long_o, pair = long_rows(re, ro, r_buf, band_a[...], alpha)
-    l_rows[pl.ds(0, HALF, 2), :] = long_e
-    l_rows[pl.ds(1, HALF, 2), :] = long_o
-    l_send[...] = l_rows[...].reshape(128, 4, N2)
+    l_send[pl.ds(0, HALF, 2), :] = long_e
+    l_send[pl.ds(1, HALF, 2), :] = long_o
     pl.semaphore_wait(ready, len(tp_peers))
     everyone = [(at[o[1:]], tp ^ o[0]) for o in all_offsets()]
+    l_dst = l_recv.at[pl.ds(pl.multiple_of(4 * my_id, 4), 4), :]
     for e, t in everyone:
-        remote(l_send.at[n_tp * e + t], l_recv.at[my_id], 5, {"ctx": e, "tp": t})
-    local(l_send.at[my_id], l_recv.at[my_id], 5)
+        src = l_send.at[pl.ds(pl.multiple_of(4 * (n_tp * e + t), 4), 4), :]
+        remote(src, l_dst, 5, {"ctx": e, "tp": t})
+    local(l_send.at[pl.ds(pl.multiple_of(4 * my_id, 4), 4), :], l_dst, 5)
 
     finish(f_buf, recv_sem.at[0])
-    fe, fo = f_buf[0], f_buf[1]
+    fe, fo = f_buf[:, 0].reshape(HALF, N2), f_buf[:, 1].reshape(HALF, N2)
     ft_hi, ft_lo = turned_filter(fe, fo)
     s_send[...] = short_row(pair, ft_hi, ft_lo, re, lam)
     for e, t in everyone:
@@ -323,29 +323,46 @@
     t_hi, t_lo = split(tail_matrix(fo[HALF - 8 :, :], band_c[...]))
     for c in range(2):
         filter_product(zf, zw, lam[c], alpha[c], zv[c])
-    even, odd = inverse_rows([inverse_mix(zg[c], zv[c], twist, mix) for c in range(2)], inv)
-    for c in range(2):
-        s = slice(c * N2, (c + 1) * N2)
-        first = recv[c, 1, :16, :]
-        fold = (dot(first, t_hi) + dot(first, t_lo))[:1, :]
-        last = jnp.concatenate([odd[: HALF - 1, s], odd[HALF - 1 :, s] + fold], axis=0)
-        rows = [x.reshape(32, 8, N2) for x in (even[:, s], last)]
-        sg_send[c] = jnp.concatenate(rows, axis=1).astype(BF16)
+    halves_sg = [inverse_mix(zg[c], zv[c], twist, mix) for c in range(2)]
     sg_dst = sg_recv.at[pl.ds(2 * me, 2)]
-    for e in peers:
-        remote(sg_send.at[:, e], sg_dst, 3, {"ctx": e})
-    local(sg_send.at[:, me], sg_dst, 3)
+    folds = [(dot(recv[c, 0, 1], t_hi) + dot(recv[c, 0, 1], t_lo))[:1, :] for c in range(2)]
+    ys = [split(jnp.concatenate([x[h] for x in halves_sg], axis=1)) for h in range(2)]
+    for p in range(2):
+        even, odd = (
+            dot(inv[r, :], twice(hi)) + dot(inv[r, :N1], lo)
+            for (hi, lo), r in zip(ys, (slice(h * HALF + 128 * p, h * HALF + 128 * (p + 1)) for h in range(2)))
+        )
+        for c in range(2):
+            s = slice(c * N2, (c + 1) * N2)
+            last = odd[:, s]
+            if p == 1:
+                last = jnp.concatenate([last[:127], last[127:] + folds[c]], axis=0)
+            rows = [x.reshape(16, 8, N2) for x in (even[:, s], last)]
+            sg_send[16 * p : 16 * (p + 1), c] = jnp.concatenate(rows, axis=1).astype(BF16)
+        for z in (2, 1, 3, 0):
+            for x in (2, 1, 3, 0):
+                e = 16 * p + ((my_z + z) & 3) * 4 + ((my_x + x) & 3)
+                if z or x:
+                    remote(sg_send.at[e], sg_dst, 3, {"ctx": e})
+                else:
+
+                    @pl.when(my_y != p)
+                    def _():
+                        remote(sg_send.at[e], sg_dst, 3, {"ctx": e})
+
+    local(sg_send.at[me], sg_dst, 3)
 
     finish(l_recv, recv_sem.at[5])
-    long_out[...] = jnp.sum(l_recv[...], axis=0)
+    total = jnp.sum(l_recv[...].reshape(64, 8, N2), axis=0)
+    long_out[...] = total[:4] + total[4:]
     finish(s_recv, recv_sem.at[6])
     short_out[...] = jnp.sum(s_recv[...], axis=0)
     finish(sg_recv, recv_sem.at[3])
-    finish(f_buf.at[:, pl.ds(0, 8 * n_peers), :], send_sem.at[0])
+    finish(f_buf.at[pl.ds(0, n_peers)], send_sem.at[0])
     for c in range(2):
         finish(send.at[pl.ds(0, n_peers)], send_sem.at[1 + c])
-    finish(sg_send.at[:, pl.ds(0, n_peers)], send_sem.at[3])
-    finish(l_send.at[pl.ds(0, n_all - 1)], send_sem.at[5])
+    finish(sg_send.at[pl.ds(0, n_peers)], send_sem.at[3])
+    finish(l_send.at[pl.ds(0, 4 * (n_all - 1)), :], send_sem.at[5])
     finish(s_recv.at[pl.ds(0, n_all - 1)], send_sem.at[6])
 
 
@@ -393,10 +410,10 @@
             V((64, 2048), BF16), V((64, 2048), BF16), V((16, N2), F32), V((2, 8, N2), F32),
             V((1, N2), F32), S((64,), F32), S((64,), F32),
             V((2 * N1, N1), BF16), V((N1, 2 * N1), BF16), V((768, 2 * N2), F32), V((1536, 256), BF16),
-            V((64, 2, 16, N2), BF16), V((2, 2, N1, N2), BF16), V((2, HALF, N2), F32),
+            V((64, 2, 16, N2), BF16), V((2, 32, 2, 16, N2), BF16), V((32, 2, 8, N2), F32),
             spec, spec, spec, spec, spec, spec, spec, V((2, N1, N2), F32), V((HALF + 8, N2), F32),
             V((768, N2), BF16), V((384, N2), BF16), spec,
-            V((N1, N2), F32), V((128, 4, N2), F32), V((128, 4, N2), F32), V((1, N2), F32), V((128, 1, N2), F32), V((2, 32, 16, N2), BF16),
+            V((N1, N2), F32), V((N1, N2), F32), V((1, N2), F32), V((128, 1, N2), F32), V((32, 2, 16, N2), BF16),
             pltpu.SemaphoreType.DMA((10,)), pltpu.SemaphoreType.DMA((7,)), pltpu.SemaphoreType.DMA((7,)),
             pltpu.SemaphoreType.REGULAR,
         ],

time: 31.1 us -> 30.7 us (0.987)
  the two profiles are of different devices: /device:TPU:0 before, /device:TPU:1 now
where the time goes in v6:
time: 30.7 us; the launch traced here: 30.5 us
  Pallas kernels  29.9 us (97%)
  between operations  0.64 us (2%)
    pallas_call x1, Pallas kernels, shards(): pl.pallas_call(lambda *refs: kernel(n_ctx, n_tp, *refs), out_shape=(pltpu...  28.9 us
    pallas_call x1, Pallas kernels, shards(): pl.pallas_call(lay_out, out_shape=(jax.ShapeDtypeStruct((64, 2048), BF16)...  0.97 us

profile of v6, /device:TPU:1, one launch (start us, length us, event | category | flops | bytes accessed | tf_op | source)
XLA Modules:
  0.0 30.5 jit_solution(11920526624034712453)
XLA Ops:
  0.6 28.9 %shard_map.121 = (bf16[64,16,128]{2,1,0:T(8,128)(2,1)S(1)}, f32[4,128]{1,0:T(4,128)S(1)}, f32[1,128]{1,0:T(1,128)S(1)}) custom-call(bf16[64,2048]{1,0:T(8,128)(2,1)} %refs_0_.1, bf16[64,2048]{1,0:T(8,128)(2,1)} %refs_1_.1, f32[16,128]{1,0:T(8,128)} %bitcast.4, f32[1,128]{1,0:T(1,128)} %bitcast.6, f32[64]{0:T(128)} %refs_4_.1, f32[64]{0:T(128)} %refs_5_.1, ...), custom_call_target="tpu_custom_call" | custom-call | flops 6000000000 | bytes 8000000 | tf_op jit(solution)/shard_map/pallas_call | solution.py:400
  29.6 1.0 %shard_map.122 = (bf16[64,2048]{1,0:T(8,128)(2,1)}, f32[4,128]{1,0:T(4,128)}, f32[1,128]{1,0:T(1,128)}) custom-call(bf16[64,16,128]{2,1,0:T(8,128)(2,1)S(1)} %get-tuple-element.9.sg_in, f32[4,128]{1,0:T(4,128)S(1)} %get-tuple-element.10.long_in, f32[1,128]{1,0:T(1,128)S(1)} %get-tuple-element.11.short_in), custom_call_target="tpu_custom_call" | custom-call | tf_op jit(solution)/shard_map/pallas_call | solution.py:428

commit v7 on v6

--- a/solution.py
+++ b/solution.py
@@ -120,8 +120,8 @@
     j = lax.broadcasted_iota(jnp.int32, (256, 256), 1)
     if back:
         i, j = j, i
-    p = i % 16
-    return one_hot((i // 16 == j % 16) & (2 * (p % 8) + p // 8 == j // 16))
+    p = i & 15
+    return one_hot(((i >> 4) == (j & 15)) & (2 * (p & 7) + (p >> 3) == (j >> 4)))
 
 
 def rolled(w_row, first, rows):
@@ -199,13 +199,13 @@
         return y + min(o[2], 4 - o[2]) + min(o[3], 4 - o[3])
 
     out = [(t, y, z, x) for y in range(2) for z in range(4) for x in range(4) for t in range(4)][1:]
-    return sorted(out, key=lambda o: -far(o))
+    return sorted(out, key=lambda o: (-(o[0] & 2), -far(o)))
 
 
 def kernel(
     n_ctx, n_tp,
     sig, cot, filt, w_in, lam_in, alpha_in, f_tab, i_tab, t_tab, m_tab,
-    sg_recv, long_out, short_out,
+    sg_recv, long_out, short_out, swap_out,
     sig_v, cot_v, filt_v, filt_s, w_v, lam_s, alpha_s, fwd, inv, twist, mix,
     send, recv, f_buf, zs0, zg0, zs1, zg1, zf, zv0, zv1, half, r_buf, band_a, band_c, zw,
     l_send, l_recv, s_send, s_recv, sg_send, load_sem, send_sem, recv_sem, ready,
@@ -254,8 +254,6 @@
         send[ch, 0] = y[:, :N2].reshape(16, 16, N2)
         send[ch, 1] = y[:, N2:].reshape(16, 16, N2)
     pl.semaphore_wait(barrier, n_peers + len(tp_peers))
-    for t in tp_peers:
-        pl.semaphore_signal(ready, inc=1, device_id={"tp": t}, device_id_type=MESH)
 
     f_dst = f_buf.at[me]
 
@@ -271,15 +269,21 @@
     def finish(ref, sem):
         pltpu.make_async_copy(ref, ref, sem).wait()
 
-    for c in range(2):
+    for e in peers:
+        remote(send.at[2 * e], recv.at[0, me], 1, {"ctx": e})
+    for q in range(2):
         for e in peers:
-            remote(send.at[2 * e + c], recv.at[c, me], 1 + c, {"ctx": e})
+            remote(send.at[2 * e + 1, q], recv.at[1, me, q], 2 + 5 * q, {"ctx": e})
     for e in peers:
         remote(filt_s, f_dst, 0, {"ctx": e})
-    for c in range(2):
-        local(send.at[2 * me + c], recv.at[c, me], 1 + c)
+    local(send.at[2 * me], recv.at[0, me], 1)
+    for q in range(2):
+        local(send.at[2 * me + 1, q], recv.at[1, me, q], 2 + 5 * q)
     local(filt_s, f_dst, 0)
 
+    for t in tp_peers:
+        pl.semaphore_signal(ready, inc=1, device_id={"tp": t}, device_id_type=MESH)
+    swap_out[...] = swap_matrix(True)
     w_row = w_v[...]
     band_a[...] = stack3(jnp.transpose(rolled(w_row, True, N2)))
     band_c[...] = stack3(rolled(w_row, False, N2)[:, :N2])
@@ -289,16 +293,16 @@
         c.wait()
     zw[...] = dot(split3(twist[:N1, :] * jnp.concatenate([w_row, w_row], axis=1)), mix[:768, :])
 
-    for c in range(2):
-        finish(recv.at[c], recv_sem.at[1 + c])
-        se, so = halves(recv[c, :, 0])
-        ge, go = halves(recv[c, :, 1])
-        forward_exact(
-            jnp.concatenate([se, ge], axis=1), jnp.concatenate([so, go], axis=1), fwd, twist, mix, (zs[c], zg[c])
-        )
-        part = inverse_mix(zg[c], zs[c], twist, mix)
-        if c == 0:
-            half[0], half[1] = part
+    finish(recv.at[0], recv_sem.at[1])
+    se, so = halves(recv[0, :, 0])
+    ge, go = halves(recv[0, :, 1])
+    forward_exact(jnp.concatenate([se, ge], axis=1), jnp.concatenate([so, go], axis=1), fwd, twist, mix, (zs0, zg0))
+    half[0], half[1] = inverse_mix(zg0, zs0, twist, mix)
+    for q, z in enumerate((zs1, zg1)):
+        finish(recv.at[1, :, q], recv_sem.at[2 + 5 * q])
+        xe, xo = halves(recv[1, :, q])
+        forward_exact(xe, xo, fwd, twist, mix, (z,))
+    part = inverse_mix(zg1, zs1, twist, mix)
     even, odd = inverse_rows([(half[0], half[1]), part], inv)
     re, ro = (even[:, :N2], even[:, N2:]), (odd[:, :N2], odd[:, N2:])
     long_e, long_o, pair = long_rows(re, ro, r_buf, band_a[...], alpha)
@@ -359,15 +363,15 @@
     short_out[...] = jnp.sum(s_recv[...], axis=0)
     finish(sg_recv, recv_sem.at[3])
     finish(f_buf.at[pl.ds(0, n_peers)], send_sem.at[0])
-    for c in range(2):
-        finish(send.at[pl.ds(0, n_peers)], send_sem.at[1 + c])
+    finish(send.at[pl.ds(0, n_peers)], send_sem.at[1])
+    for q in range(2):
+        finish(send.at[pl.ds(0, n_peers), q], send_sem.at[2 + 5 * q])
     finish(sg_send.at[pl.ds(0, n_peers)], send_sem.at[3])
     finish(l_send.at[pl.ds(0, 4 * (n_all - 1)), :], send_sem.at[5])
     finish(s_recv.at[pl.ds(0, n_all - 1)], send_sem.at[6])
 
 
-def lay_out(sg_in, long_in, short_in, sg_out, long_out, short_out, rows, sem):
-    swap = swap_matrix(True)
+def lay_out(sg_in, long_in, short_in, swap_in, sg_out, long_out, short_out, rows, sem):
     copies = [
         pltpu.make_async_copy(long_in, long_out, sem.at[2]),
         pltpu.make_async_copy(short_in, short_out, sem.at[3]),
@@ -378,7 +382,7 @@
         x = jnp.concatenate(
             [sg_in[32 * g + 16 * h : 32 * g + 16 * (h + 1)].reshape(256, N2) for h in range(2)], axis=1
         )
-        y = dot(swap, x).astype(BF16)
+        y = dot(swap_in[...], x).astype(BF16)
         for h in range(2):
             ch = slice(32 * g + 16 * h, 32 * g + 16 * (h + 1))
             for a in range(16):
@@ -403,9 +407,10 @@
             pltpu.VMEM((64, 16, N2), BF16),
             pltpu.VMEM((4, N2), F32),
             pltpu.VMEM((1, N2), F32),
+            pltpu.VMEM((256, 256), BF16),
         ),
         in_specs=[hbm] * 10,
-        out_specs=(vmem, vmem, vmem),
+        out_specs=(vmem, vmem, vmem, vmem),
         scratch_shapes=[
             V((64, 2048), BF16), V((64, 2048), BF16), V((16, N2), F32), V((2, 8, N2), F32),
             V((1, N2), F32), S((64,), F32), S((64,), F32),
@@ -414,7 +419,7 @@
             spec, spec, spec, spec, spec, spec, spec, V((2, N1, N2), F32), V((HALF + 8, N2), F32),
             V((768, N2), BF16), V((384, N2), BF16), spec,
             V((N1, N2), F32), V((N1, N2), F32), V((1, N2), F32), V((128, 1, N2), F32), V((32, 2, 16, N2), BF16),
-            pltpu.SemaphoreType.DMA((10,)), pltpu.SemaphoreType.DMA((7,)), pltpu.SemaphoreType.DMA((7,)),
+            pltpu.SemaphoreType.DMA((10,)), pltpu.SemaphoreType.DMA((8,)), pltpu.SemaphoreType.DMA((8,)),
             pltpu.SemaphoreType.REGULAR,
         ],
         compiler_params=pltpu.CompilerParams(
@@ -432,7 +437,7 @@
             jax.ShapeDtypeStruct((4, N2), F32),
             jax.ShapeDtypeStruct((1, N2), F32),
         ),
-        in_specs=[vmem, vmem, vmem],
+        in_specs=[vmem, vmem, vmem, vmem],
         out_specs=(hbm, hbm, hbm),
         scratch_shapes=[V((64, 2048), BF16), pltpu.SemaphoreType.DMA((4,))],
     )(*[pltpu.with_memory_space_constraint(r, pltpu.VMEM) for r in raw])

time: 30.7 us -> 30.8 us (level)
  no operation moved by 1% of the time
where the time goes in v7:
time: 30.8 us; the launch traced here: 30.5 us
  Pallas kernels  29.8 us (97%)
  between operations  0.64 us (2%)
    pallas_call x1, Pallas kernels, shards(): pl.pallas_call(lambda *refs: kernel(n_ctx, n_tp, *refs), out_shape=(pltpu...  28.9 us
    pallas_call x1, Pallas kernels, shards(): pl.pallas_call(lay_out, out_shape=(jax.ShapeDtypeStruct((64, 2048), BF16)...  0.96 us

profile of v7, /device:TPU:1, one launch (start us, length us, event | category | flops | bytes accessed | tf_op | source)
XLA Modules:
  0.0 30.5 jit_solution(13607667434179266825)
XLA Ops:
  0.6 28.9 %shard_map.121 = (bf16[64,16,128]{2,1,0:T(8,128)(2,1)S(1)}, f32[4,128]{1,0:T(4,128)S(1)}, f32[1,128]{1,0:T(1,128)S(1)}, bf16[256,256]{1,0:T(8,128)(2,1)S(1)}) custom-call(bf16[64,2048]{1,0:T(8,128)(2,1)} %refs_0_.1, bf16[64,2048]{1,0:T(8,128)(2,1)} %refs_1_.1, f32[16,128]{1,0:T(8,128)} %bitcast.4, f32[1,128]{1,0:T(1,128)} %bitcast.6, f32[64]{0:T(128)} %refs_4_.1, ...), custom_call_target="tpu_custom_call" | custom-call | flops 6000000000 | bytes 8000000 | tf_op jit(solution)/shard_map/pallas_call | solution.py:404
  29.5 1.0 %shard_map.122 = (bf16[64,2048]{1,0:T(8,128)(2,1)}, f32[4,128]{1,0:T(4,128)}, f32[1,128]{1,0:T(1,128)}) custom-call(bf16[64,16,128]{2,1,0:T(8,128)(2,1)S(1)} %get-tuple-element.10.sg_in, f32[4,128]{1,0:T(4,128)S(1)} %get-tuple-element.11.long_in, f32[1,128]{1,0:T(1,128)S(1)} %get-tuple-element.12.short_in, bf16[256,256]{1,0:T(8,128)(2,1)S(1)} %get-tuple-element.13.swap_in), custom_call_target="tpu_custom_call" | custom-call | tf_op jit(solution)/shard_map/pallas_call | solution.py:433

commit v8 on v6

--- a/solution.py
+++ b/solution.py
@@ -135,16 +135,12 @@
     return jnp.concatenate([hi, hi, lo], axis=0)
 
 
-def long_rows(re, ro, r_buf, band, alpha):
+def row_pairs(re, ro, r_buf):
     se, so = re[0] + re[1], ro[0] + ro[1]
     r_buf[:HALF, :] = se
-    pair = jnp.concatenate(
+    return jnp.concatenate(
         [jnp.concatenate([se, so], axis=1), jnp.concatenate([so, r_buf[pl.ds(1, HALF), :]], axis=1)], axis=0
     )
-    long = dot(split3(pair), band)
-    long_e = long[:HALF] + (alpha[0] * re[0] + alpha[1] * re[1])
-    long_o = long[HALF:] + (alpha[0] * ro[0] + alpha[1] * ro[1])
-    return long_e, long_o, pair
 
 
 def turned_filter(fe, fo):
@@ -301,15 +297,31 @@
             half[0], half[1] = part
     even, odd = inverse_rows([(half[0], half[1]), part], inv)
     re, ro = (even[:, :N2], even[:, N2:]), (odd[:, :N2], odd[:, N2:])
-    long_e, long_o, pair = long_rows(re, ro, r_buf, band_a[...], alpha)
-    l_send[pl.ds(0, HALF, 2), :] = long_e
-    l_send[pl.ds(1, HALF, 2), :] = long_o
+    pair = row_pairs(re, ro, r_buf)
     pl.semaphore_wait(ready, len(tp_peers))
     everyone = [(at[o[1:]], tp ^ o[0]) for o in all_offsets()]
     l_dst = l_recv.at[pl.ds(pl.multiple_of(4 * my_id, 4), 4), :]
-    for e, t in everyone:
-        src = l_send.at[pl.ds(pl.multiple_of(4 * (n_tp * e + t), 4), 4), :]
-        remote(src, l_dst, 5, {"ctx": e, "tp": t})
+    steps = sorted(
+        [(t, z, x) for t in range(4) for z in range(4) for x in range(4)],
+        key=lambda o: -((o[0] & 2) + min(o[1], 4 - o[1]) + min(o[2], 4 - o[2])),
+    )
+    for p in range(2):
+        m = slice(128 * p, 128 * (p + 1))
+        m2 = slice(HALF + 128 * p, HALF + 128 * (p + 1))
+        rows = dot(split3(jnp.concatenate([pair[m], pair[m2]], axis=0)), band_a[...])
+        l_send[pl.ds(HALF * p, 128, 2), :] = rows[:128] + (alpha[0] * re[0][m] + alpha[1] * re[1][m])
+        l_send[pl.ds(HALF * p + 1, 128, 2), :] = rows[128:] + (alpha[0] * ro[0][m] + alpha[1] * ro[1][m])
+        for t, z, x in steps:
+            e = 16 * p + ((my_z + z) & 3) * 4 + ((my_x + x) & 3)
+            src = l_send.at[pl.ds(pl.multiple_of(4 * (n_tp * e + (tp ^ t)), 4), 4), :]
+            if t or z or x:
+                remote(src, l_dst, 5, {"ctx": e, "tp": tp ^ t})
+            else:
+
+                @pl.when(my_y != p)
+                def _():
+                    remote(src, l_dst, 5, {"ctx": e, "tp": tp ^ t})
+
     local(l_send.at[pl.ds(pl.multiple_of(4 * my_id, 4), 4), :], l_dst, 5)
 
     finish(f_buf, recv_sem.at[0])

time: 30.7 us -> 31 us (level)
  no operation moved by 1% of the time
where the time goes in v8:
time: 31 us; the launch traced here: 30.7 us
  Pallas kernels  30.1 us (97%)
  between operations  0.64 us (2%)
    pallas_call x1, Pallas kernels, shards(): pl.pallas_call(lambda *refs: kernel(n_ctx, n_tp, *refs), out_shape=(pltpu...  29.1 us
    pallas_call x1, Pallas kernels, shards(): pl.pallas_call(lay_out, out_shape=(jax.ShapeDtypeStruct((64, 2048), BF16)...  0.97 us

profile of v8, /device:TPU:1, one launch (start us, length us, event | category | flops | bytes accessed | tf_op | source)
XLA Modules:
  0.0 30.7 jit_solution(9420453460102252305)
XLA Ops:
  0.6 29.1 %shard_map.121 = (bf16[64,16,128]{2,1,0:T(8,128)(2,1)S(1)}, f32[4,128]{1,0:T(4,128)S(1)}, f32[1,128]{1,0:T(1,128)S(1)}) custom-call(bf16[64,2048]{1,0:T(8,128)(2,1)} %refs_0_.1, bf16[64,2048]{1,0:T(8,128)(2,1)} %refs_1_.1, f32[16,128]{1,0:T(8,128)} %bitcast.4, f32[1,128]{1,0:T(1,128)} %bitcast.6, f32[64]{0:T(128)} %refs_4_.1, f32[64]{0:T(128)} %refs_5_.1, ...), custom_call_target="tpu_custom_call" | custom-call | flops 6000000000 | bytes 8000000 | tf_op jit(solution)/shard_map/pallas_call | solution.py:412
  29.7 1.0 %shard_map.122 = (bf16[64,2048]{1,0:T(8,128)(2,1)}, f32[4,128]{1,0:T(4,128)}, f32[1,128]{1,0:T(1,128)}) custom-call(bf16[64,16,128]{2,1,0:T(8,128)(2,1)S(1)} %get-tuple-element.9.sg_in, f32[4,128]{1,0:T(4,128)S(1)} %get-tuple-element.10.long_in, f32[1,128]{1,0:T(1,128)S(1)} %get-tuple-element.11.short_in), custom_call_target="tpu_custom_call" | custom-call | tf_op jit(solution)/shard_map/pallas_call | solution.py:440
